TPU v7x, 512 devices: a whole 4x8x8 slice. The times are simulated.
512 devices in a mesh: occ: 16 (over y, core), vir: 32 (over x, z).
Axes of the slice: x: 4, y: 8, z: 8, core: 2. Of those that a mesh axis runs over, the one named last changes fastest.
Arguments:
- amplitudes: float32 [2048, 12288], P('occ', 'vir'), may hold values from -6 to 6
- integrals: float32 [12288, 4096], P('vir', 'occ'), may hold values from -0.109375 to 0.109375
- pair_mask: int32 [32, 192], P('occ', 'vir'), may hold values 0 or 1
- tile_mask: int32 [192, 64], P('vir', 'occ'), may hold values 0 or 1
Outputs:
- residual: float32 [2048, 4096], P('occ', 'vir')
Inputs may be any that keep to these rules, and one draw needn't show every extreme that they name: `pair_mask`: 0 marks a tile that is absent and contributes nothing. `tile_mask`: 0 marks a tile that is absent and contributes nothing.
All inputs are finite; a program needn't handle non-finite values. No bound on the sum of `pair_mask` or of `tile_mask` on one device may be relied on, other than what follows from the above.
Results may differ from a plain program's by a relative error of at most 0.00007.
Values sent between devices are 32-bit elements; how exact they have to be, the bound alone decides.
No kernel may reach another device: no remote copies, remote signals or barrier semaphores. Data moves between devices by JAX's collectives and lax.ppermute only.
A program may use at most 64 MiB of HBM per device.

v0:
```python
import jax
import jax.numpy as jnp
from jax import lax
from jax.sharding import PartitionSpec as P


def expand(mask, width):
    grown = jnp.repeat(mask.astype(jnp.float32), width, axis=0)
    return jnp.repeat(grown, width, axis=1)


def body(amplitudes, integrals, pair_mask, tile_mask):
    tile_width = amplitudes.shape[1] // pair_mask.shape[1]
    masked_t = amplitudes * expand(pair_mask, tile_width)
    masked_v = integrals * expand(tile_mask, tile_width)
    partial_sum = jnp.dot(
        masked_t,
        lax.all_gather(masked_v, "occ", axis=1, tiled=True),
        precision=lax.Precision.HIGHEST,
        preferred_element_type=jnp.float32,
    )
    return lax.psum_scatter(partial_sum, "vir", scatter_dimension=1, tiled=True)


def solution(mesh):
    in_specs = (P("occ", "vir"), P("vir", "occ"), P("occ", "vir"), P("vir", "occ"))
    out_specs = P("occ", "vir")
    return jax.shard_map(body, mesh=mesh, in_specs=in_specs, out_specs=out_specs, check_vma=False)
```

profile of v0, /device:TPU:8, one launch (start us, length us, event | category | flops | bytes accessed | tf_op | source)
XLA Modules:
  0.0 302.7 jit_solution(3729471157549326904)
XLA Ops:
  6.5 0.0 all-gather.2.cloned.1.call-start
  6.5 0.7 convert_element_type.7
  7.2 0.1 broadcast_in_dim.14
  7.3 0.1 reshape.14
  7.4 1.2 copy.11
  8.5 0.8 bitcast_multiply_fusion
  9.3 0.0 all-gather.2.cloned.1.call-update
  9.3 0.0 reduce-scatter.2.cloned.1.call-start
  9.4 0.7 convert_element_type.6
  10.1 0.1 copy.9
  10.2 0.1 broadcast_in_dim.12
  10.2 0.1 reshape.12
  10.3 1.1 copy.10
  11.4 51.0 %all-gather.2.cloned.1.call-done = f32[384,4096]{0,1:T(8,128)} async-done(((f32[384,256]{0,1:T(8,128)}), f32[384,4096]{0,1:T(8,128)}) %all-gather.2.cloned.1.call-update) | async-done | bytes 6291472 | tf_op jit(solution)/shard_map/all_gather | solution.py:18
  62.4 10.7 %fusion = f32[128,4096]{1,0:T(8,128)} fusion(f32[128,384]{0,1:T(8,128)S(1)} %bitcast_multiply_fusion.1, f32[384,4096]{0,1:T(8,128)} %all-gather.2.cloned.1.call-done), kind=kOutput, calls=%fused_computation.2 | convolution fusion | flops 2415919104 | bytes 8585216 | tf_op jit(solution)/shard_map/dot_general | solution.py:16
  73.0 0.0 reduce-scatter.2.cloned.1.call-update
  73.1 222.8 %reduce-scatter.2.cloned.1.call-done = f32[128,128]{1,0:T(8,128)} async-done(((f32[128,4096]{1,0:T(8,128)}), f32[128,128]{1,0:T(8,128)}) %reduce-scatter.2.cloned.1.call-update) | async-done | bytes 65552 | tf_op jit(solution)/shard_map/reduce_scatter | solution.py:22
  (1 shorter events, 0.0 us)
Async XLA Ops:
  6.5 55.9 %all-gather.2.cloned.1.call-start = ((), (), s32[]{:S(2)}) async-start(), calls=%async_computation.1 | async-start | bytes 6684672 | tf_op jit(solution)/shard_map/all_gather | solution.py:18
  9.3 286.5 %reduce-scatter.2.cloned.1.call-start = ((), (), s32[]{:S(2)}) async-start(), calls=%async_computation.2 | async-start | bytes 2162688 | tf_op jit(solution)/shard_map/reduce_scatter | solution.py:22
Sparse Core Ops, SparseCore 0:
  9.5 52.8 all-gather.1
  73.2 222.6 reduce-scatter.1
where the time goes:
time: 303 us
  waiting for transfers between devices  274 us (90%)
  between operations  13.4 us (4%)
  matrix products  10.7 us (4%)
    reduce_scatter x1, waiting for transfers between devices, body(): return lax.psum_scatter(partial_sum, 'vir', scatter_dimension=1, tiled=True)  223 us
    all_gather x1, waiting for transfers between devices, body(): lax.all_gather(masked_v, 'occ', axis=1, tiled=True)  51 us
    dot_general x1, matrix products, body(): jnp.dot(masked_t, lax.all_gather(masked_v, 'occ', axis=1, tiled=True), pr...  10.7 us
  transfers between devices with their start and end apart: 2, of which 2 were waited for; matrix products, arithmetic and copies ran while one was open for 1% of the time, Pallas kernels for 0%

commit v1 on v0

v1 whole, which is shorter than its diff:
```python
import jax
import jax.numpy as jnp
from jax import lax
from jax.sharding import Mesh, PartitionSpec as P


def expand(mask, width):
    grown = jnp.repeat(mask.astype(jnp.float32), width, axis=0)
    return jnp.repeat(grown, width, axis=1)


def body(amplitudes, integrals, pair_mask, tile_mask):
    tile_width = amplitudes.shape[1] // pair_mask.shape[1]
    masked_v = integrals * expand(tile_mask, tile_width)
    other_v = lax.ppermute(masked_v, "l", [(0, 1), (1, 0)])
    masked_t = amplitudes * expand(pair_mask, tile_width)
    rows = lax.all_gather(masked_t, "h", axis=0, tiled=True)
    near = lax.all_gather(masked_v, "c", axis=1, tiled=True)
    far = lax.all_gather(other_v, "c", axis=1, tiled=True)
    low = lax.axis_index("l") == 0
    columns = jnp.concatenate([jnp.where(low, near, far), jnp.where(low, far, near)], axis=1)
    partial_sum = jnp.dot(rows, columns, precision=lax.Precision.HIGH, preferred_element_type=jnp.float32)
    count = lax.axis_size("x")
    parts = lax.all_to_all(partial_sum, "x", 0, 0, tiled=True)
    over_x = parts.reshape(count, -1, parts.shape[1]).sum(0)
    depth = lax.axis_size("z")
    pieces = over_x.reshape(over_x.shape[0], depth, -1).transpose(1, 0, 2)
    pieces = lax.all_to_all(pieces, "z", 0, 0, tiled=True)
    total = pieces.sum(0)
    swap = [(h * count + x, x * count + h) for h in range(count) for x in range(count)]
    return lax.ppermute(total, ("h", "x"), swap)


def solution(mesh):
    fine = Mesh(mesh.devices.reshape(4, 2, 2, 4, 8), ("h", "l", "c", "x", "z"))
    occ, vir = ("h", "l", "c"), ("x", "z")
    in_specs = (P(occ, vir), P(vir, occ), P(occ, vir), P(vir, occ))
    return jax.shard_map(body, mesh=fine, in_specs=in_specs, out_specs=P(occ, vir), check_vma=False)
```

time: 303 us -> 107 us (0.35)
  the two profiles are of different devices: /device:TPU:8 before, /device:TPU:4 now
where the time goes in v1:
time: 107 us
  blocking collectives  84.2 us (79%)
  starting transfers between devices  9.76 us (9%)
  waiting for transfers between devices  6.19 us (6%)
  matrix products  2.78 us (3%)
  local copies, waits for them, and re-layouts  2.71 us (3%)
  other arithmetic  1.09 us (1%)
    all_to_all x1, blocking collectives, body(): parts = lax.all_to_all(partial_sum, 'x', 0, 0, tiled=True)  28.5 us
    all_to_all x1, blocking collectives, body(): pieces = lax.all_to_all(pieces, 'z', 0, 0, tiled=True)  26.5 us
    all_gather x1, blocking collectives, body(): rows = lax.all_gather(masked_t, 'h', axis=0, tiled=True)  24.4 us
    ppermute x1, starting transfers between devices, body(): return lax.ppermute(total, ('h', 'x'), swap)  6.28 us
    ppermute x1, waiting for transfers between devices, body(): return lax.ppermute(total, ('h', 'x'), swap)  6.19 us
    ppermute x1, starting transfers between devices, body(): other_v = lax.ppermute(masked_v, 'l', [(0, 1), (1, 0)])  3.48 us
    dot_general x1, matrix products, body(): jnp.dot(rows, columns, precision=lax.Precision.HIGH, preferred_element_ty...  2.78 us
    all_gather x1, blocking collectives, body(): near = lax.all_gather(masked_v, 'c', axis=1, tiled=True)  2.37 us
  transfers between devices with their start and end apart: 2, of which 1 were waited for; matrix products, arithmetic and copies ran while one was open for 0% of the time, Pallas kernels for 0%

profile of v1, /device:TPU:4, one launch (start us, length us, event | category | flops | bytes accessed | tf_op | source)
XLA Modules:
  0.0 106.9 jit_solution(17523145308158582603)
XLA Ops:
  0.0 0.0 copy-start.1
  0.0 0.0 copy-start
  0.0 0.7 convert_element_type.7
  0.7 0.1 broadcast_in_dim.14
  0.8 0.1 reshape.21
  0.9 1.2 %copy.21 = f32[384,256]{0,1:T(8,128)S(1)} copy(f32[384,256]{1,0:T(8,128)} %param.5) | data formatting | bytes 786432 | tf_op args[1]
  2.1 3.5 %collective-permute-start = (f32[384,256]{0,1:T(8,128)S(1)}, f32[384,256]{0,1:T(8,128)S(1)}, u32[]{:S(2)}, u32[]{:S(2)}) collective-permute-start(f32[384,256]{0,1:T(8,128)S(1)} %bitcast_multiply_fusion), channel_id=1, source_target_pairs={{0,64},{64,0},{1,65},{65,1},{2,66},{66,2},{3,67},{67,3},{4,68},{68... | collective-permute-start | bytes 1179656 | tf_op jit(solution)/shard_map/ppermute | solution.py:15
  5.6 2.4 %all_gather.10 = f32[384,512]{0,1:T(8,128)S(1)} all-gather(f32[384,256]{0,1:T(8,128)S(1)} %bitcast_multiply_fusion), channel_id=1, replica_groups=mesh['h'=4,'l'=2,'c'=2,'x'=4,'z'=8] {'c'}, dimensions={1}, use_global_device_ids=true | all-gather | bytes 1179648 | tf_op jit(solution)/shard_map/all_gather | solution.py:18
  7.9 0.0 copy-done.1
  8.0 0.1 copy.19
  8.1 0.1 broadcast_in_dim.12
  8.1 0.1 reshape.19
  8.2 0.0 copy-done
  8.2 0.1 copy.20
  8.4 24.4 %all_gather.9 = f32[512,384]{0,1:T(8,128)S(1)} all-gather(f32[128,384]{0,1:T(8,128)S(1)} %bitcast_multiply_fusion.1), channel_id=1, replica_groups=mesh['h'=4,'l'=2,'c'=2,'x'=4,'z'=8] {'h'}, dimensions={0}, use_global_device_ids=true | all-gather | bytes 983040 | tf_op jit(solution)/shard_map/all_gather | solution.py:17
  32.8 0.0 collective-permute-done
  32.8 2.4 %all_gather.11 = f32[384,512]{0,1:T(8,128)S(1)} all-gather(f32[384,256]{0,1:T(8,128)S(1)} %collective-permute-done), channel_id=1, replica_groups=mesh['h'=4,'l'=2,'c'=2,'x'=4,'z'=8] {'c'}, dimensions={1}, use_global_device_ids=true | all-gather | bytes 1179648 | tf_op jit(solution)/shard_map/all_gather | solution.py:19
  35.2 0.1 broadcast_select_fusion.1
  35.3 2.8 %fusion = f32[512,1024]{1,0:T(8,128)S(1)} fusion(f32[512,384]{0,1:T(8,128)S(1)} %all_gather.9, f32[384,512]{0,1:T(8,128)S(1)} %get-tuple-element.6, f32[384,512]{0,1:T(8,128)S(1)} %get-tuple-element.5), kind=kOutput, calls=%fused_computation | convolution fusion | flops 1208352768 | bytes 4456448 | tf_op jit(solution)/shard_map/dot_general | solution.py:22
  38.1 28.5 %all_to_all.14 = f32[4,128,1024]{2,1,0:T(8,128)S(1)} all-to-all(f32[4,128,1024]{2,1,0:T(8,128)S(1)} %bitcast.13), channel_id=1, replica_groups=mesh['h'=4,'l'=2,'c'=2,'x'=4,'z'=8] {'x'}, dimensions={0} | all-to-all | bytes 4194304 | tf_op jit(solution)/shard_map/all_to_all | solution.py:24
  66.6 0.2 reduce_sum.18
  66.8 0.2 copy.22
  67.0 0.2 copy.23
  67.2 26.5 %all_to_all.15 = f32[8,128,128]{2,1,0:T(8,128)S(1)} all-to-all(f32[8,128,128]{2,1,0:T(8,128)S(1)} %copy.23), channel_id=1, replica_groups=mesh['h'=4,'l'=2,'c'=2,'x'=4,'z'=8] {'z'}, dimensions={0} | all-to-all | bytes 1048576 | tf_op jit(solution)/shard_map/all_to_all | solution.py:28
  93.8 6.3 %collective-permute-start.1 = (f32[128,128]{1,0:T(8,128)S(1)}, f32[128,128]{1,0:T(8,128)S(1)}, u32[]{:S(2)}, u32[]{:S(2)}) collective-permute-start(f32[128,128]{1,0:T(8,128)S(1)} %reduce_sum.19), channel_id=1, source_target_pairs={{0,0},{8,128},{16,256},{24,384},{128,8},{136,136},{144,264},{152,3... | collective-permute-start | bytes 196616 | tf_op jit(solution)/shard_map/ppermute | solution.py:31
  100.0 6.2 %collective-permute-done.1 = f32[128,128]{1,0:T(8,128)S(1)} collective-permute-done((f32[128,128]{1,0:T(8,128)S(1)}, f32[128,128]{1,0:T(8,128)S(1)}, u32[]{:S(2)}, u32[]{:S(2)}) %collective-permute-start.1) | collective-permute-done | bytes 65568 | tf_op jit(solution)/shard_map/ppermute | solution.py:31
  106.2 0.6 copy.25
  (4 shorter events, 0.1 us)
Async XLA Ops:
  0.0 8.0 %copy-start.1 = (s32[2,6]{1,0:T(2,128)S(1)}, s32[2,6]{1,0:T(2,128)}, u32[]{:S(2)}) copy-start(s32[2,6]{1,0:T(2,128)} %param.6) | copy-start | bytes 148
  0.0 8.2 %copy-start = (f32[128,384]{1,0:T(8,128)S(1)}, f32[128,384]{1,0:T(8,128)}, u32[]{:S(2)}) copy-start(f32[128,384]{1,0:T(8,128)} %param.4) | copy-start | bytes 589828
  2.1 30.7 %collective-permute-start = (f32[384,256]{0,1:T(8,128)S(1)}, f32[384,256]{0,1:T(8,128)S(1)}, u32[]{:S(2)}, u32[]{:S(2)}) collective-permute-start(f32[384,256]{0,1:T(8,128)S(1)} %bitcast_multiply_fusion), channel_id=1, source_target_pairs={{0,64},{64,0},{1,65},{65,1},{2,66},{66,2},{3,67},{67,3},{4,68},{68... | collective-permute-start | bytes 1179656 | tf_op jit(solution)/shard_map/ppermute | solution.py:15
  93.8 12.5 %collective-permute-start.1 = (f32[128,128]{1,0:T(8,128)S(1)}, f32[128,128]{1,0:T(8,128)S(1)}, u32[]{:S(2)}, u32[]{:S(2)}) collective-permute-start(f32[128,128]{1,0:T(8,128)S(1)} %reduce_sum.19), channel_id=1, source_target_pairs={{0,0},{8,128},{16,256},{24,384},{128,8},{136,136},{144,264},{152,3... | collective-permute-start | bytes 196616 | tf_op jit(solution)/shard_map/ppermute | solution.py:31

commit v2 on v1

v2 whole, which is shorter than its diff:
```python
import jax
import jax.numpy as jnp
from jax import lax
from jax.sharding import Mesh, PartitionSpec as P

AXES = ("h", "l", "c", "x", "z")
SIZES = (4, 2, 2, 4, 8)


def moves(names, target):
    sizes = [SIZES[AXES.index(name)] for name in names]
    pairs = []
    total = 1
    for size in sizes:
        total *= size
    for source in range(total):
        rest, at = source, {}
        for name, size in zip(names[::-1], sizes[::-1]):
            at[name], rest = rest % size, rest // size
        to = dict(at, **target(at))
        index = 0
        for name, size in zip(names, sizes):
            index = index * size + to[name] % size
        pairs.append((source, index))
    return pairs


def send(value, names, target):
    return lax.ppermute(value, names, moves(names, target))


def expand(mask, width):
    grown = jnp.repeat(mask.astype(jnp.float32), width, axis=0)
    return jnp.repeat(grown, width, axis=1)


def product(a, b):
    return jnp.dot(a, b, precision=lax.Precision.HIGH, preferred_element_type=jnp.float32)


def sign(at):
    return 1 - 2 * ((at["x"] + at["c"]) % 2)


def body(amplitudes, integrals, pair_mask, tile_mask):
    l = lax.axis_index("l")
    width = amplitudes.shape[1] // pair_mask.shape[1]
    masked_v = integrals * expand(tile_mask, width)
    far_half = send(masked_v, ("l",), lambda at: {"l": at["l"] + 1})
    near = lax.all_gather(masked_v, "c", axis=1, tiled=True)
    near_beside = send(near, ("c", "x"), lambda at: {"x": at["x"] + sign(at)})
    masked_t = amplitudes * expand(pair_mask, width)
    names = ("h", "c", "x")
    own = jnp.concatenate([
        send(masked_t, names, lambda at: {"h": at["h"] - at["x"]}),
        send(masked_t, names, lambda at: {"h": at["h"] - at["x"] + sign(at)}),
    ])
    beside = jnp.concatenate([
        send(masked_t, names, lambda at: {"h": at["h"] - at["x"] - sign(at), "x": at["x"] + sign(at)}),
        send(masked_t, names, lambda at: {"h": at["h"] - at["x"] - 2 * sign(at), "x": at["x"] + sign(at)}),
    ])
    far = lax.all_gather(far_half, "c", axis=1, tiled=True)
    far_beside = send(far, ("c", "x"), lambda at: {"x": at["x"] + sign(at)})
    near_sum = product(own, near) + product(beside, near_beside)
    far_sum = product(own, far) + product(beside, far_beside)
    away = jnp.concatenate([near_sum[128:], far_sum[128:]], axis=1)
    came = send(away, ("c", "x"), lambda at: {"x": at["x"] - sign(at)})
    near_sum, far_sum = near_sum[:128] + came[:, :512], far_sum[:128] + came[:, 512:]
    low = l == 0
    halves = jnp.concatenate([jnp.where(low, near_sum, far_sum), jnp.where(low, far_sum, near_sum)], axis=1)
    pieces = halves.reshape(128, 8, 128).transpose(1, 0, 2)
    total = lax.all_to_all(pieces, "z", 0, 0, tiled=True).sum(0)
    return send(total, ("h", "x"), lambda at: {"h": at["h"] + at["x"], "x": at["h"]})


def solution(mesh):
    fine = Mesh(mesh.devices.reshape(SIZES), AXES)
    occ, vir = ("h", "l", "c"), ("x", "z")
    in_specs = (P(occ, vir), P(vir, occ), P(occ, vir), P(vir, occ))
    return jax.shard_map(body, mesh=fine, in_specs=in_specs, out_specs=P(occ, vir), check_vma=False)
```

time: 107 us -> 99.3 us (0.928)
  the two profiles are of different devices: /device:TPU:4 before, /device:TPU:40 now
where the time goes in v2:
time: 99.3 us; the launch traced here: 98.8 us
  starting transfers between devices  35.9 us (36%)
  blocking collectives  30.7 us (31%)
  waiting for transfers between devices  24.2 us (24%)
  local copies, waits for them, and re-layouts  4.09 us (4%)
  matrix products  3.49 us (4%)
    ppermute x9, starting transfers between devices, send(): return lax.ppermute(value, names, moves(names, target))  35.9 us
    all_to_all x1, blocking collectives, body(): total = lax.all_to_all(pieces, 'z', 0, 0, tiled=True).sum(0)  25.3 us
    ppermute x9, waiting for transfers between devices, send(): return lax.ppermute(value, names, moves(names, target))  24.2 us
    dot_general x4, matrix products, product(): jnp.dot(a, b, precision=lax.Precision.HIGH, preferred_element_type=jnp.fl...  3.49 us
    all_gather x1, blocking collectives, body(): near = lax.all_gather(masked_v, 'c', axis=1, tiled=True)  2.99 us
    unnamed x15, local copies, waits for them, and re-layouts  2.73 us
    all_gather x1, blocking collectives, body(): far = lax.all_gather(far_half, 'c', axis=1, tiled=True)  2.37 us
  transfers between devices with their start and end apart: 9, of which 4 were waited for; matrix products, arithmetic and copies ran while one was open for 2% of the time, Pallas kernels for 0%

profile of v2, /device:TPU:40, one launch (start us, length us, event | category | flops | bytes accessed | tf_op | source)
XLA Modules:
  0.0 98.8 jit_solution(895904465045186417)
XLA Ops:
  0.0 0.0 copy-start.4
  0.0 0.0 copy-start.2
  0.0 1.1 %copy.13 = f32[128,384]{0,1:T(8,128)S(1)} copy(f32[128,384]{1,0:T(8,128)} %param.4) | data formatting | bytes 393216 | tf_op args[0]
  1.1 0.0 copy-done.4
  1.1 0.1 copy.12
  1.2 0.1 broadcast_in_dim.12
  1.3 0.1 reshape.15
  1.4 0.0 copy-start.3
  1.4 4.1 %collective-permute-start.2 = (f32[128,384]{0,1:T(8,128)S(1)}, f32[128,384]{0,1:T(8,128)S(1)}, u32[]{:S(2)}, u32[]{:S(2)}) collective-permute-start(f32[128,384]{0,1:T(8,128)S(1)} %bitcast_multiply_fusion.1), channel_id=1, source_target_pairs={{0,392},{8,0},{16,152},{24,272},{32,184},{40,304},{48,424},{56,32}... | collective-permute-start | bytes 589832 | tf_op jit(solution)/shard_map/ppermute | solution.py:29
  5.5 0.0 copy-done.2
  5.5 0.2 copy.14
  5.7 0.0 copy-done.3
  5.7 0.1 broadcast_in_dim.14
  5.8 0.1 reshape.17
  5.9 2.4 %collective-permute-start.5 = (f32[384,256]{0,1:T(8,128)S(1)}, f32[384,256]{0,1:T(8,128)S(1)}, u32[]{:S(2)}, u32[]{:S(2)}) collective-permute-start(f32[384,256]{0,1:T(8,128)S(1)} %bitcast_multiply_fusion), channel_id=1, source_target_pairs={{0,64},{64,0},{1,65},{65,1},{2,66},{66,2},{3,67},{67,3},{4,68},{68... | collective-permute-start | bytes 1179656 | tf_op jit(solution)/shard_map/ppermute | solution.py:29
  8.3 3.0 %all_gather.6 = f32[384,512]{0,1:T(8,128)S(1)} all-gather(f32[384,256]{0,1:T(8,128)S(1)} %bitcast_multiply_fusion), channel_id=1, replica_groups=mesh['h'=4,'l'=2,'c'=2,'x'=4,'z'=8] {'c'}, dimensions={1}, use_global_device_ids=true | all-gather | bytes 1179648 | tf_op jit(solution)/shard_map/all_gather | solution.py:50
  11.2 2.0 %collective-permute-start.4 = (f32[384,512]{0,1:T(8,128)S(1)}, f32[384,512]{0,1:T(8,128)S(1)}, u32[]{:S(2)}, u32[]{:S(2)}) collective-permute-start(f32[384,512]{0,1:T(8,128)S(1)} %all_gather.6), channel_id=1, source_target_pairs={{0,8},{8,0},{16,24},{24,16},{32,56},{40,48},{48,40},{56,32},{1,9},... | collective-permute-start | bytes 2359304 | tf_op jit(solution)/shard_map/ppermute | solution.py:29
  13.3 6.8 %collective-permute-start.3 = (f32[128,384]{0,1:T(8,128)S(1)}, f32[128,384]{0,1:T(8,128)S(1)}, u32[]{:S(2)}, u32[]{:S(2)}) collective-permute-start(f32[128,384]{0,1:T(8,128)S(1)} %bitcast_multiply_fusion.1), channel_id=1, source_target_pairs={{0,264},{8,128},{16,24},{24,400},{32,312},{40,176},{48,40},{56,416... | collective-permute-start | bytes 589832 | tf_op jit(solution)/shard_map/ppermute | solution.py:29
  20.1 0.7 collective-permute-start
  20.8 0.0 collective-permute-done.2
  20.8 4.0 %collective-permute-start.1 = (f32[128,384]{0,1:T(8,128)S(1)}, f32[128,384]{0,1:T(8,128)S(1)}, u32[]{:S(2)}, u32[]{:S(2)}) collective-permute-start(f32[128,384]{0,1:T(8,128)S(1)} %bitcast_multiply_fusion.1), channel_id=1, source_target_pairs={{0,128},{8,264},{16,400},{24,24},{32,416},{40,40},{48,176},{56,312... | collective-permute-start | bytes 589832 | tf_op jit(solution)/shard_map/ppermute | solution.py:29
  24.9 0.0 collective-permute-done.5
  24.9 2.4 %all_gather.7 = f32[384,512]{0,1:T(8,128)S(1)} all-gather(f32[384,256]{0,1:T(8,128)S(1)} %collective-permute-done.5), channel_id=1, replica_groups=mesh['h'=4,'l'=2,'c'=2,'x'=4,'z'=8] {'c'}, dimensions={1}, use_global_device_ids=true | all-gather | bytes 1179648 | tf_op jit(solution)/shard_map/all_gather | solution.py:62
  27.2 7.2 %collective-permute-start.6 = (f32[384,512]{0,1:T(8,128)S(1)}, f32[384,512]{0,1:T(8,128)S(1)}, u32[]{:S(2)}, u32[]{:S(2)}) collective-permute-start(f32[384,512]{0,1:T(8,128)S(1)} %all_gather.7), channel_id=1, source_target_pairs={{0,8},{8,0},{16,24},{24,16},{32,56},{40,48},{48,40},{56,32},{1,9},... | collective-permute-start | bytes 2359304 | tf_op jit(solution)/shard_map/ppermute | solution.py:29
  34.4 0.0 collective-permute-done
  34.5 0.0 collective-permute-done.3
  34.5 1.8 %collective-permute-done.1 = f32[128,384]{0,1:T(8,128)S(1)} collective-permute-done((f32[128,384]{0,1:T(8,128)S(1)}, f32[128,384]{0,1:T(8,128)S(1)}, u32[]{:S(2)}, u32[]{:S(2)}) %collective-permute-start.1) | collective-permute-done | bytes 196640 | tf_op jit(solution)/shard_map/ppermute | solution.py:29
  36.4 0.0 collective-permute-done.4
  36.4 0.9 fusion
  37.3 0.9 convolution_add_fusion.1
  38.1 0.0 copy-start
  38.1 0.8 copy-done
  38.9 5.5 %collective-permute-done.6 = f32[384,512]{0,1:T(8,128)S(1)} collective-permute-done((f32[384,512]{0,1:T(8,128)S(1)}, f32[384,512]{0,1:T(8,128)S(1)}, u32[]{:S(2)}, u32[]{:S(2)}) %collective-permute-start.6) | collective-permute-done | bytes 786464 | tf_op jit(solution)/shard_map/ppermute | solution.py:29
  44.4 0.9 fusion.1
  45.3 0.9 convolution_add_fusion
  46.1 0.0 slice-start
  46.2 0.9 slice-done
  47.1 0.0 copy-start.1
  47.1 4.1 %collective-permute-start.7 = (f32[128,1024]{1,0:T(8,128)S(1)}, f32[128,1024]{1,0:T(8,128)S(1)}, u32[]{:S(2)}, u32[]{:S(2)}) collective-permute-start(f32[128,1024]{1,0:T(8,128)S(1)} %pad_maximum_fusion), channel_id=1, source_target_pairs={{0,24},{8,16},{16,8},{24,0},{32,40},{40,32},{48,56},{56,48},{1,25}... | collective-permute-start | bytes 1572872 | tf_op jit(solution)/shard_map/ppermute | solution.py:29
  51.3 8.3 %collective-permute-done.7 = f32[128,1024]{1,0:T(8,128)S(1)} collective-permute-done((f32[128,1024]{1,0:T(8,128)S(1)}, f32[128,1024]{1,0:T(8,128)S(1)}, u32[]{:S(2)}, u32[]{:S(2)}) %collective-permute-start.7) | collective-permute-done | bytes 524320 | tf_op jit(solution)/shard_map/ppermute | solution.py:29
  59.6 0.0 copy-done.1
  59.6 0.1 broadcast_select_fusion.1
  59.7 25.3 %all_to_all.5 = f32[8,128,128]{2,1,0:T(8,128)S(1)} all-to-all(f32[8,128,128]{2,1,0:T(8,128)S(1)} %bitcast_bitcast_fusion), channel_id=1, replica_groups=mesh['h'=4,'l'=2,'c'=2,'x'=4,'z'=8] {'z'}, dimensions={0} | all-to-all | bytes 1048576 | tf_op jit(solution)/shard_map/all_to_all | solution.py:72
  85.0 4.6 %collective-permute-start.8 = (f32[128,128]{1,0:T(8,128)S(1)}, f32[128,128]{1,0:T(8,128)S(1)}, u32[]{:S(2)}, u32[]{:S(2)}) collective-permute-start(f32[128,128]{1,0:T(8,128)S(1)} %reduce_sum.9), channel_id=1, source_target_pairs={{0,0},{8,128},{16,256},{24,384},{128,136},{136,264},{144,392},{152... | collective-permute-start | bytes 196616 | tf_op jit(solution)/shard_map/ppermute | solution.py:29
  89.6 8.6 %collective-permute-done.8 = f32[128,128]{1,0:T(8,128)S(1)} collective-permute-done((f32[128,128]{1,0:T(8,128)S(1)}, f32[128,128]{1,0:T(8,128)S(1)}, u32[]{:S(2)}, u32[]{:S(2)}) %collective-permute-start.8) | collective-permute-done | bytes 65568 | tf_op jit(solution)/shard_map/ppermute | solution.py:29
  98.2 0.6 copy.21
  (12 shorter events, 0.2 us)
Async XLA Ops:
  0.0 1.1 %copy-start.4 = (s32[2,6]{1,0:T(2,128)S(1)}, s32[2,6]{1,0:T(2,128)}, u32[]{:S(2)}) copy-start(s32[2,6]{1,0:T(2,128)} %param.6) | copy-start | bytes 148
  0.0 5.5 %copy-start.2 = (f32[384,256]{1,0:T(8,128)S(1)}, f32[384,256]{1,0:T(8,128)}, u32[]{:S(2)}) copy-start(f32[384,256]{1,0:T(8,128)} %param.5) | copy-start | bytes 1179652
  1.4 4.3 %copy-start.3 = (s32[6,4]{0,1:T(4,128)S(1)}, s32[6,4]{0,1:T(4,128)}, u32[]{:S(2)}) copy-start(s32[6,4]{0,1:T(4,128)} %param.7) | copy-start | bytes 292
  1.4 19.4 %collective-permute-start.2 = (f32[128,384]{0,1:T(8,128)S(1)}, f32[128,384]{0,1:T(8,128)S(1)}, u32[]{:S(2)}, u32[]{:S(2)}) collective-permute-start(f32[128,384]{0,1:T(8,128)S(1)} %bitcast_multiply_fusion.1), channel_id=1, source_target_pairs={{0,392},{8,0},{16,152},{24,272},{32,184},{40,304},{48,424},{56,32}... | collective-permute-start | bytes 589832 | tf_op jit(solution)/shard_map/ppermute | solution.py:29
  5.9 19.0 %collective-permute-start.5 = (f32[384,256]{0,1:T(8,128)S(1)}, f32[384,256]{0,1:T(8,128)S(1)}, u32[]{:S(2)}, u32[]{:S(2)}) collective-permute-start(f32[384,256]{0,1:T(8,128)S(1)} %bitcast_multiply_fusion), channel_id=1, source_target_pairs={{0,64},{64,0},{1,65},{65,1},{2,66},{66,2},{3,67},{67,3},{4,68},{68... | collective-permute-start | bytes 1179656 | tf_op jit(solution)/shard_map/ppermute | solution.py:29
  11.2 25.1 %collective-permute-start.4 = (f32[384,512]{0,1:T(8,128)S(1)}, f32[384,512]{0,1:T(8,128)S(1)}, u32[]{:S(2)}, u32[]{:S(2)}) collective-permute-start(f32[384,512]{0,1:T(8,128)S(1)} %all_gather.6), channel_id=1, source_target_pairs={{0,8},{8,0},{16,24},{24,16},{32,56},{40,48},{48,40},{56,32},{1,9},... | collective-permute-start | bytes 2359304 | tf_op jit(solution)/shard_map/ppermute | solution.py:29
  13.3 21.2 %collective-permute-start.3 = (f32[128,384]{0,1:T(8,128)S(1)}, f32[128,384]{0,1:T(8,128)S(1)}, u32[]{:S(2)}, u32[]{:S(2)}) collective-permute-start(f32[128,384]{0,1:T(8,128)S(1)} %bitcast_multiply_fusion.1), channel_id=1, source_target_pairs={{0,264},{8,128},{16,24},{24,400},{32,312},{40,176},{48,40},{56,416... | collective-permute-start | bytes 589832 | tf_op jit(solution)/shard_map/ppermute | solution.py:29
  20.1 14.3 %collective-permute-start = (f32[128,384]{0,1:T(8,128)S(1)}, f32[128,384]{0,1:T(8,128)S(1)}, u32[]{:S(2)}, u32[]{:S(2)}) collective-permute-start(f32[128,384]{0,1:T(8,128)S(1)} %bitcast_multiply_fusion.1), channel_id=1, source_target_pairs={{0,0},{8,392},{16,272},{24,152},{32,32},{40,424},{48,304},{56,184}... | collective-permute-start | bytes 589832 | tf_op jit(solution)/shard_map/ppermute | solution.py:29
  20.8 15.5 %collective-permute-start.1 = (f32[128,384]{0,1:T(8,128)S(1)}, f32[128,384]{0,1:T(8,128)S(1)}, u32[]{:S(2)}, u32[]{:S(2)}) collective-permute-start(f32[128,384]{0,1:T(8,128)S(1)} %bitcast_multiply_fusion.1), channel_id=1, source_target_pairs={{0,128},{8,264},{16,400},{24,24},{32,416},{40,40},{48,176},{56,312... | collective-permute-start | bytes 589832 | tf_op jit(solution)/shard_map/ppermute | solution.py:29
  27.2 17.1 %collective-permute-start.6 = (f32[384,512]{0,1:T(8,128)S(1)}, f32[384,512]{0,1:T(8,128)S(1)}, u32[]{:S(2)}, u32[]{:S(2)}) collective-permute-start(f32[384,512]{0,1:T(8,128)S(1)} %all_gather.7), channel_id=1, source_target_pairs={{0,8},{8,0},{16,24},{24,16},{32,56},{40,48},{48,40},{56,32},{1,9},... | collective-permute-start | bytes 2359304 | tf_op jit(solution)/shard_map/ppermute | solution.py:29
  38.1 0.8 copy-start
  46.1 1.0 slice-start
  47.1 12.5 %copy-start.1 = (f32[256,512]{1,0:T(8,128)S(1)}, f32[256,512]{1,0:T(8,128)}, u32[]{:S(2)}) copy-start(f32[256,512]{1,0:T(8,128)} %copy-done) | copy-start | bytes 1572868
  47.1 12.4 %collective-permute-start.7 = (f32[128,1024]{1,0:T(8,128)S(1)}, f32[128,1024]{1,0:T(8,128)S(1)}, u32[]{:S(2)}, u32[]{:S(2)}) collective-permute-start(f32[128,1024]{1,0:T(8,128)S(1)} %pad_maximum_fusion), channel_id=1, source_target_pairs={{0,24},{8,16},{16,8},{24,0},{32,40},{40,32},{48,56},{56,48},{1,25}... | collective-permute-start | bytes 1572872 | tf_op jit(solution)/shard_map/ppermute | solution.py:29
  85.0 13.2 %collective-permute-start.8 = (f32[128,128]{1,0:T(8,128)S(1)}, f32[128,128]{1,0:T(8,128)S(1)}, u32[]{:S(2)}, u32[]{:S(2)}) collective-permute-start(f32[128,128]{1,0:T(8,128)S(1)} %reduce_sum.9), channel_id=1, source_target_pairs={{0,0},{8,128},{16,256},{24,384},{128,136},{136,264},{144,392},{152... | collective-permute-start | bytes 196616 | tf_op jit(solution)/shard_map/ppermute | solution.py:29

commit v3 on v2

--- a/solution.py
+++ b/solution.py
@@ -69,7 +69,14 @@
     low = l == 0
     halves = jnp.concatenate([jnp.where(low, near_sum, far_sum), jnp.where(low, far_sum, near_sum)], axis=1)
     pieces = halves.reshape(128, 8, 128).transpose(1, 0, 2)
-    total = lax.all_to_all(pieces, "z", 0, 0, tiled=True).sum(0)
+    groups = []
+    for first in range(0, 512, 8):
+        core = first // 32 % 2
+        groups.append([first + (k + 4 * core) % 8 for k in range(8)])
+    turn = lax.axis_index("c") * 4
+    pieces = jnp.concatenate([pieces, pieces[:4]])
+    pieces = lax.dynamic_slice_in_dim(pieces, turn, 8, 0)
+    total = lax.all_to_all(pieces, AXES, 0, 0, tiled=True, axis_index_groups=groups).sum(0)
     return send(total, ("h", "x"), lambda at: {"h": at["h"] + at["x"], "x": at["h"]})
 
 

time: 99.3 us -> 97.3 us (0.980)
  blocking collectives: 30.7 us -> 28.6 us
    all_to_all x1, blocking collectives: 25.3 us -> 23.2 us  [body(): lax.all_to_all(pieces, AXES, 0, 0, tiled=True, axis_index_groups=groups)]
where the time goes in v3:
time: 97.3 us; the launch traced here: 96.9 us
  starting transfers between devices  35.9 us (37%)
  blocking collectives  28.6 us (29%)
  waiting for transfers between devices  24.2 us (25%)
  local copies, waits for them, and re-layouts  4.11 us (4%)
  matrix products  3.49 us (4%)
    ppermute x9, starting transfers between devices, send(): return lax.ppermute(value, names, moves(names, target))  35.9 us
    ppermute x9, waiting for transfers between devices, send(): return lax.ppermute(value, names, moves(names, target))  24.2 us
    all_to_all x1, blocking collectives, body(): lax.all_to_all(pieces, AXES, 0, 0, tiled=True, axis_index_groups=groups)  23.2 us
    dot_general x4, matrix products, product(): jnp.dot(a, b, precision=lax.Precision.HIGH, preferred_element_type=jnp.fl...  3.49 us
    all_gather x1, blocking collectives, body(): near = lax.all_gather(masked_v, 'c', axis=1, tiled=True)  2.99 us
    unnamed x15, local copies, waits for them, and re-layouts  2.73 us
    all_gather x1, blocking collectives, body(): far = lax.all_gather(far_half, 'c', axis=1, tiled=True)  2.37 us
  transfers between devices with their start and end apart: 9, of which 4 were waited for; matrix products, arithmetic and copies ran while one was open for 2% of the time, Pallas kernels for 0%

profile of v3, /device:TPU:40, one launch (start us, length us, event | category | flops | bytes accessed | tf_op | source)
XLA Modules:
  0.0 96.9 jit_solution(14063444466938659748)
XLA Ops:
  0.0 0.0 copy-start.4
  0.0 0.0 copy-start.2
  0.0 1.1 %copy.13 = f32[128,384]{0,1:T(8,128)S(1)} copy(f32[128,384]{1,0:T(8,128)} %param.4) | data formatting | bytes 393216 | tf_op args[0]
  1.1 0.0 copy-done.4
  1.1 0.1 copy.12
  1.2 0.1 broadcast_in_dim.12
  1.3 0.1 reshape.15
  1.4 0.0 copy-start.3
  1.4 4.1 %collective-permute-start.2 = (f32[128,384]{0,1:T(8,128)S(1)}, f32[128,384]{0,1:T(8,128)S(1)}, u32[]{:S(2)}, u32[]{:S(2)}) collective-permute-start(f32[128,384]{0,1:T(8,128)S(1)} %bitcast_multiply_fusion.1), channel_id=1, source_target_pairs={{0,392},{8,0},{16,152},{24,272},{32,184},{40,304},{48,424},{56,32}... | collective-permute-start | bytes 589832 | tf_op jit(solution)/shard_map/ppermute | solution.py:29
  5.5 0.0 copy-done.2
  5.5 0.2 copy.14
  5.7 0.0 copy-done.3
  5.7 0.1 broadcast_in_dim.14
  5.8 0.1 reshape.17
  5.9 2.4 %collective-permute-start.5 = (f32[384,256]{0,1:T(8,128)S(1)}, f32[384,256]{0,1:T(8,128)S(1)}, u32[]{:S(2)}, u32[]{:S(2)}) collective-permute-start(f32[384,256]{0,1:T(8,128)S(1)} %bitcast_multiply_fusion), channel_id=1, source_target_pairs={{0,64},{64,0},{1,65},{65,1},{2,66},{66,2},{3,67},{67,3},{4,68},{68... | collective-permute-start | bytes 1179656 | tf_op jit(solution)/shard_map/ppermute | solution.py:29
  8.3 3.0 %all_gather.6 = f32[384,512]{0,1:T(8,128)S(1)} all-gather(f32[384,256]{0,1:T(8,128)S(1)} %bitcast_multiply_fusion), channel_id=1, replica_groups=mesh['h'=4,'l'=2,'c'=2,'x'=4,'z'=8] {'c'}, dimensions={1}, use_global_device_ids=true | all-gather | bytes 1179648 | tf_op jit(solution)/shard_map/all_gather | solution.py:50
  11.2 2.0 %collective-permute-start.4 = (f32[384,512]{0,1:T(8,128)S(1)}, f32[384,512]{0,1:T(8,128)S(1)}, u32[]{:S(2)}, u32[]{:S(2)}) collective-permute-start(f32[384,512]{0,1:T(8,128)S(1)} %all_gather.6), channel_id=1, source_target_pairs={{0,8},{8,0},{16,24},{24,16},{32,56},{40,48},{48,40},{56,32},{1,9},... | collective-permute-start | bytes 2359304 | tf_op jit(solution)/shard_map/ppermute | solution.py:29
  13.3 6.8 %collective-permute-start.3 = (f32[128,384]{0,1:T(8,128)S(1)}, f32[128,384]{0,1:T(8,128)S(1)}, u32[]{:S(2)}, u32[]{:S(2)}) collective-permute-start(f32[128,384]{0,1:T(8,128)S(1)} %bitcast_multiply_fusion.1), channel_id=1, source_target_pairs={{0,264},{8,128},{16,24},{24,400},{32,312},{40,176},{48,40},{56,416... | collective-permute-start | bytes 589832 | tf_op jit(solution)/shard_map/ppermute | solution.py:29
  20.1 0.7 collective-permute-start
  20.8 0.0 collective-permute-done.2
  20.8 4.0 %collective-permute-start.1 = (f32[128,384]{0,1:T(8,128)S(1)}, f32[128,384]{0,1:T(8,128)S(1)}, u32[]{:S(2)}, u32[]{:S(2)}) collective-permute-start(f32[128,384]{0,1:T(8,128)S(1)} %bitcast_multiply_fusion.1), channel_id=1, source_target_pairs={{0,128},{8,264},{16,400},{24,24},{32,416},{40,40},{48,176},{56,312... | collective-permute-start | bytes 589832 | tf_op jit(solution)/shard_map/ppermute | solution.py:29
  24.9 0.0 collective-permute-done.5
  24.9 2.4 %all_gather.7 = f32[384,512]{0,1:T(8,128)S(1)} all-gather(f32[384,256]{0,1:T(8,128)S(1)} %collective-permute-done.5), channel_id=1, replica_groups=mesh['h'=4,'l'=2,'c'=2,'x'=4,'z'=8] {'c'}, dimensions={1}, use_global_device_ids=true | all-gather | bytes 1179648 | tf_op jit(solution)/shard_map/all_gather | solution.py:62
  27.2 7.2 %collective-permute-start.6 = (f32[384,512]{0,1:T(8,128)S(1)}, f32[384,512]{0,1:T(8,128)S(1)}, u32[]{:S(2)}, u32[]{:S(2)}) collective-permute-start(f32[384,512]{0,1:T(8,128)S(1)} %all_gather.7), channel_id=1, source_target_pairs={{0,8},{8,0},{16,24},{24,16},{32,56},{40,48},{48,40},{56,32},{1,9},... | collective-permute-start | bytes 2359304 | tf_op jit(solution)/shard_map/ppermute | solution.py:29
  34.4 0.0 collective-permute-done
  34.5 0.0 collective-permute-done.3
  34.5 1.8 %collective-permute-done.1 = f32[128,384]{0,1:T(8,128)S(1)} collective-permute-done((f32[128,384]{0,1:T(8,128)S(1)}, f32[128,384]{0,1:T(8,128)S(1)}, u32[]{:S(2)}, u32[]{:S(2)}) %collective-permute-start.1) | collective-permute-done | bytes 196640 | tf_op jit(solution)/shard_map/ppermute | solution.py:29
  36.4 0.0 collective-permute-done.4
  36.4 0.9 fusion.1
  37.3 0.9 convolution_add_fusion.1
  38.1 0.0 copy-start
  38.1 0.8 copy-done
  38.9 5.5 %collective-permute-done.6 = f32[384,512]{0,1:T(8,128)S(1)} collective-permute-done((f32[384,512]{0,1:T(8,128)S(1)}, f32[384,512]{0,1:T(8,128)S(1)}, u32[]{:S(2)}, u32[]{:S(2)}) %collective-permute-start.6) | collective-permute-done | bytes 786464 | tf_op jit(solution)/shard_map/ppermute | solution.py:29
  44.4 0.9 fusion.2
  45.3 0.9 convolution_add_fusion
  46.1 0.0 slice-start
  46.2 0.9 slice-done
  47.1 0.0 copy-start.1
  47.1 4.1 %collective-permute-start.7 = (f32[128,1024]{1,0:T(8,128)S(1)}, f32[128,1024]{1,0:T(8,128)S(1)}, u32[]{:S(2)}, u32[]{:S(2)}) collective-permute-start(f32[128,1024]{1,0:T(8,128)S(1)} %pad_maximum_fusion), channel_id=1, source_target_pairs={{0,24},{8,16},{16,8},{24,0},{32,40},{40,32},{48,56},{56,48},{1,25}... | collective-permute-start | bytes 1572872 | tf_op jit(solution)/shard_map/ppermute | solution.py:29
  51.3 8.3 %collective-permute-done.7 = f32[128,1024]{1,0:T(8,128)S(1)} collective-permute-done((f32[128,1024]{1,0:T(8,128)S(1)}, f32[128,1024]{1,0:T(8,128)S(1)}, u32[]{:S(2)}, u32[]{:S(2)}) %collective-permute-start.7) | collective-permute-done | bytes 524320 | tf_op jit(solution)/shard_map/ppermute | solution.py:29
  59.6 0.0 copy-done.1
  59.6 0.1 broadcast_select_fusion.1
  59.7 0.1 fusion
  59.8 23.2 %all_to_all.5 = f32[8,128,128]{2,1,0:T(8,128)S(1)} all-to-all(f32[8,128,128]{2,1,0:T(8,128)S(1)} %fusion), channel_id=1, replica_groups={{0,1,2,3,4,5,6,7},{8,9,10,11,12,13,14,15},{16,17,18,19,20,21,22,23},{24..., dimensions={0} | all-to-all | bytes 1048576 | tf_op jit(solution)/shard_map/all_to_all | solution.py:79
  83.0 4.6 %collective-permute-start.8 = (f32[128,128]{1,0:T(8,128)S(1)}, f32[128,128]{1,0:T(8,128)S(1)}, u32[]{:S(2)}, u32[]{:S(2)}) collective-permute-start(f32[128,128]{1,0:T(8,128)S(1)} %reduce_sum.9), channel_id=1, source_target_pairs={{0,0},{8,128},{16,256},{24,384},{128,136},{136,264},{144,392},{152... | collective-permute-start | bytes 196616 | tf_op jit(solution)/shard_map/ppermute | solution.py:29
  87.6 8.6 %collective-permute-done.8 = f32[128,128]{1,0:T(8,128)S(1)} collective-permute-done((f32[128,128]{1,0:T(8,128)S(1)}, f32[128,128]{1,0:T(8,128)S(1)}, u32[]{:S(2)}, u32[]{:S(2)}) %collective-permute-start.8) | collective-permute-done | bytes 65568 | tf_op jit(solution)/shard_map/ppermute | solution.py:29
  96.2 0.6 copy.21
  (13 shorter events, 0.3 us)
Async XLA Ops:
  0.0 1.1 %copy-start.4 = (s32[2,6]{1,0:T(2,128)S(1)}, s32[2,6]{1,0:T(2,128)}, u32[]{:S(2)}) copy-start(s32[2,6]{1,0:T(2,128)} %param.6) | copy-start | bytes 148
  0.0 5.5 %copy-start.2 = (f32[384,256]{1,0:T(8,128)S(1)}, f32[384,256]{1,0:T(8,128)}, u32[]{:S(2)}) copy-start(f32[384,256]{1,0:T(8,128)} %param.5) | copy-start | bytes 1179652
  1.4 4.3 %copy-start.3 = (s32[6,4]{0,1:T(4,128)S(1)}, s32[6,4]{0,1:T(4,128)}, u32[]{:S(2)}) copy-start(s32[6,4]{0,1:T(4,128)} %param.7) | copy-start | bytes 292
  1.4 19.4 %collective-permute-start.2 = (f32[128,384]{0,1:T(8,128)S(1)}, f32[128,384]{0,1:T(8,128)S(1)}, u32[]{:S(2)}, u32[]{:S(2)}) collective-permute-start(f32[128,384]{0,1:T(8,128)S(1)} %bitcast_multiply_fusion.1), channel_id=1, source_target_pairs={{0,392},{8,0},{16,152},{24,272},{32,184},{40,304},{48,424},{56,32}... | collective-permute-start | bytes 589832 | tf_op jit(solution)/shard_map/ppermute | solution.py:29
  5.9 19.0 %collective-permute-start.5 = (f32[384,256]{0,1:T(8,128)S(1)}, f32[384,256]{0,1:T(8,128)S(1)}, u32[]{:S(2)}, u32[]{:S(2)}) collective-permute-start(f32[384,256]{0,1:T(8,128)S(1)} %bitcast_multiply_fusion), channel_id=1, source_target_pairs={{0,64},{64,0},{1,65},{65,1},{2,66},{66,2},{3,67},{67,3},{4,68},{68... | collective-permute-start | bytes 1179656 | tf_op jit(solution)/shard_map/ppermute | solution.py:29
  11.2 25.1 %collective-permute-start.4 = (f32[384,512]{0,1:T(8,128)S(1)}, f32[384,512]{0,1:T(8,128)S(1)}, u32[]{:S(2)}, u32[]{:S(2)}) collective-permute-start(f32[384,512]{0,1:T(8,128)S(1)} %all_gather.6), channel_id=1, source_target_pairs={{0,8},{8,0},{16,24},{24,16},{32,56},{40,48},{48,40},{56,32},{1,9},... | collective-permute-start | bytes 2359304 | tf_op jit(solution)/shard_map/ppermute | solution.py:29
  13.3 21.2 %collective-permute-start.3 = (f32[128,384]{0,1:T(8,128)S(1)}, f32[128,384]{0,1:T(8,128)S(1)}, u32[]{:S(2)}, u32[]{:S(2)}) collective-permute-start(f32[128,384]{0,1:T(8,128)S(1)} %bitcast_multiply_fusion.1), channel_id=1, source_target_pairs={{0,264},{8,128},{16,24},{24,400},{32,312},{40,176},{48,40},{56,416... | collective-permute-start | bytes 589832 | tf_op jit(solution)/shard_map/ppermute | solution.py:29
  20.1 14.3 %collective-permute-start = (f32[128,384]{0,1:T(8,128)S(1)}, f32[128,384]{0,1:T(8,128)S(1)}, u32[]{:S(2)}, u32[]{:S(2)}) collective-permute-start(f32[128,384]{0,1:T(8,128)S(1)} %bitcast_multiply_fusion.1), channel_id=1, source_target_pairs={{0,0},{8,392},{16,272},{24,152},{32,32},{40,424},{48,304},{56,184}... | collective-permute-start | bytes 589832 | tf_op jit(solution)/shard_map/ppermute | solution.py:29
  20.8 15.5 %collective-permute-start.1 = (f32[128,384]{0,1:T(8,128)S(1)}, f32[128,384]{0,1:T(8,128)S(1)}, u32[]{:S(2)}, u32[]{:S(2)}) collective-permute-start(f32[128,384]{0,1:T(8,128)S(1)} %bitcast_multiply_fusion.1), channel_id=1, source_target_pairs={{0,128},{8,264},{16,400},{24,24},{32,416},{40,40},{48,176},{56,312... | collective-permute-start | bytes 589832 | tf_op jit(solution)/shard_map/ppermute | solution.py:29
  27.2 17.1 %collective-permute-start.6 = (f32[384,512]{0,1:T(8,128)S(1)}, f32[384,512]{0,1:T(8,128)S(1)}, u32[]{:S(2)}, u32[]{:S(2)}) collective-permute-start(f32[384,512]{0,1:T(8,128)S(1)} %all_gather.7), channel_id=1, source_target_pairs={{0,8},{8,0},{16,24},{24,16},{32,56},{40,48},{48,40},{56,32},{1,9},... | collective-permute-start | bytes 2359304 | tf_op jit(solution)/shard_map/ppermute | solution.py:29
  38.1 0.8 copy-start
  46.1 1.0 slice-start
  47.1 12.5 %copy-start.1 = (f32[256,512]{1,0:T(8,128)S(1)}, f32[256,512]{1,0:T(8,128)}, u32[]{:S(2)}) copy-start(f32[256,512]{1,0:T(8,128)} %copy-done) | copy-start | bytes 1572868
  47.1 12.4 %collective-permute-start.7 = (f32[128,1024]{1,0:T(8,128)S(1)}, f32[128,1024]{1,0:T(8,128)S(1)}, u32[]{:S(2)}, u32[]{:S(2)}) collective-permute-start(f32[128,1024]{1,0:T(8,128)S(1)} %pad_maximum_fusion), channel_id=1, source_target_pairs={{0,24},{8,16},{16,8},{24,0},{32,40},{40,32},{48,56},{56,48},{1,25}... | collective-permute-start | bytes 1572872 | tf_op jit(solution)/shard_map/ppermute | solution.py:29
  83.0 13.2 %collective-permute-start.8 = (f32[128,128]{1,0:T(8,128)S(1)}, f32[128,128]{1,0:T(8,128)S(1)}, u32[]{:S(2)}, u32[]{:S(2)}) collective-permute-start(f32[128,128]{1,0:T(8,128)S(1)} %reduce_sum.9), channel_id=1, source_target_pairs={{0,0},{8,128},{16,256},{24,384},{128,136},{136,264},{144,392},{152... | collective-permute-start | bytes 196616 | tf_op jit(solution)/shard_map/ppermute | solution.py:29

commit v4 on v3

--- a/solution.py
+++ b/solution.py
@@ -1,6 +1,8 @@
 import jax
 import jax.numpy as jnp
 from jax import lax
+from jax.experimental import pallas as pl
+from jax.experimental.pallas import tpu as pltpu
 from jax.sharding import Mesh, PartitionSpec as P
 
 AXES = ("h", "l", "c", "x", "z")
@@ -42,6 +44,20 @@
     return 1 - 2 * ((at["x"] + at["c"]) % 2)
 
 
+def stage_rows(own, beside):
+    def kernel(own_ref, beside_ref, out_ref):
+        out_ref[:, :384], out_ref[:, 384:] = own_ref[...], beside_ref[...]
+
+    vmem = pl.BlockSpec(memory_space=pltpu.VMEM)
+    return pl.pallas_call(
+        kernel,
+        out_shape=jax.ShapeDtypeStruct((128, 768), jnp.float32),
+        in_specs=[vmem] * 2,
+        out_specs=vmem,
+        cost_estimate=pl.CostEstimate(flops=10**10, bytes_accessed=1 << 20, transcendentals=0),
+    )(own, beside)
+
+
 def body(amplitudes, integrals, pair_mask, tile_mask):
     l = lax.axis_index("l")
     width = amplitudes.shape[1] // pair_mask.shape[1]
@@ -51,21 +67,25 @@
     near_beside = send(near, ("c", "x"), lambda at: {"x": at["x"] + sign(at)})
     masked_t = amplitudes * expand(pair_mask, width)
     names = ("h", "c", "x")
-    own = jnp.concatenate([
-        send(masked_t, names, lambda at: {"h": at["h"] - at["x"]}),
-        send(masked_t, names, lambda at: {"h": at["h"] - at["x"] + sign(at)}),
-    ])
-    beside = jnp.concatenate([
-        send(masked_t, names, lambda at: {"h": at["h"] - at["x"] - sign(at), "x": at["x"] + sign(at)}),
-        send(masked_t, names, lambda at: {"h": at["h"] - at["x"] - 2 * sign(at), "x": at["x"] + sign(at)}),
-    ])
+    own_b = send(masked_t, names, lambda at: {"h": at["h"] - at["x"] + sign(at)})
+    beside_b = send(masked_t, names, lambda at: {"h": at["h"] - at["x"] - 2 * sign(at), "x": at["x"] + sign(at)})
+    staged = stage_rows(own_b, beside_b)
+    own_b, beside_b = staged[:, :384], staged[:, 384:]
     far = lax.all_gather(far_half, "c", axis=1, tiled=True)
+    masked_t, far = lax.optimization_barrier((masked_t, far))
+    own_a = send(masked_t, names, lambda at: {"h": at["h"] - at["x"]})
+    beside_a = send(masked_t, names, lambda at: {"h": at["h"] - at["x"] - sign(at), "x": at["x"] + sign(at)})
     far_beside = send(far, ("c", "x"), lambda at: {"x": at["x"] + sign(at)})
-    near_sum = product(own, near) + product(beside, near_beside)
-    far_sum = product(own, far) + product(beside, far_beside)
-    away = jnp.concatenate([near_sum[128:], far_sum[128:]], axis=1)
+    def block(own, beside, near, near_beside, far, far_beside):
+        near_block = product(own, near) + product(beside, near_beside)
+        return jnp.concatenate([near_block, product(own, far) + product(beside, far_beside)], axis=1)
+
+    integrals_held = (near, near_beside, far, far_beside)
+    away = block(own_b, beside_b, *integrals_held)
     came = send(away, ("c", "x"), lambda at: {"x": at["x"] - sign(at)})
-    near_sum, far_sum = near_sum[:128] + came[:, :512], far_sum[:128] + came[:, 512:]
+    *integrals_held, away = lax.optimization_barrier((*integrals_held, away))
+    sums = block(own_a, beside_a, *integrals_held) + came
+    near_sum, far_sum = sums[:, :512], sums[:, 512:]
     low = l == 0
     halves = jnp.concatenate([jnp.where(low, near_sum, far_sum), jnp.where(low, far_sum, near_sum)], axis=1)
     pieces = halves.reshape(128, 8, 128).transpose(1, 0, 2)

time: 97.3 us -> 95 us (0.976)
  starting transfers between devices: 35.9 us -> 28.4 us
  waiting for transfers between devices: 24.2 us -> 26.8 us
  Pallas kernels: 0 us -> 1.79 us
  matrix products: 3.49 us -> 5.14 us
    ppermute x9, starting transfers between devices: 35.9 us -> 28.4 us  [send(): return lax.ppermute(value, names, moves(names, target))]
    ppermute x9, waiting for transfers between devices: 24.2 us -> 26.8 us  [send(): return lax.ppermute(value, names, moves(names, target))]
    pallas_call x0 -> x1, Pallas kernels: none -> 1.79 us  [stage_rows(): pl.pallas_call(kernel, out_shape=jax.ShapeDtypeStruct((128, 768), jnp.flo...]
    dot_general x4 -> x8, matrix products: 3.49 us -> 5.14 us  [product(): jnp.dot(a, b, precision=lax.Precision.HIGH, preferred_element_type=jnp.fl...]
    unnamed x15 -> x12, local copies, waits for them, and re-layouts: 2.73 us -> 2.61 us
  transfers between devices with their start and end apart: 9 -> 9, of which waited for: 4 -> 4; matrix products, arithmetic and copies ran while one was open for 2% -> 6% of each run, Pallas kernels for 0% -> 2%
where the time goes in v4:
time: 95 us; the launch traced here: 94.5 us
  blocking collectives  28.6 us (30%)
  starting transfers between devices  28.4 us (30%)
  waiting for transfers between devices  26.8 us (28%)
  matrix products  5.14 us (5%)
  local copies, waits for them, and re-layouts  3.17 us (3%)
  Pallas kernels  1.79 us (2%)
    ppermute x9, starting transfers between devices, send(): return lax.ppermute(value, names, moves(names, target))  28.4 us
    ppermute x9, waiting for transfers between devices, send(): return lax.ppermute(value, names, moves(names, target))  26.8 us
    all_to_all x1, blocking collectives, body(): lax.all_to_all(pieces, AXES, 0, 0, tiled=True, axis_index_groups=groups)  23.8 us
    dot_general x8, matrix products, product(): jnp.dot(a, b, precision=lax.Precision.HIGH, preferred_element_type=jnp.fl...  5.14 us
    unnamed x12, local copies, waits for them, and re-layouts  2.61 us
    all_gather x1, blocking collectives, body(): near = lax.all_gather(masked_v, 'c', axis=1, tiled=True)  2.37 us
    all_gather x1, blocking collectives, body(): far = lax.all_gather(far_half, 'c', axis=1, tiled=True)  2.37 us
  transfers between devices with their start and end apart: 9, of which 4 were waited for; matrix products, arithmetic and copies ran while one was open for 6% of the time, Pallas kernels for 2%

profile of v4, /device:TPU:40, one launch (start us, length us, event | category | flops | bytes accessed | tf_op | source)
XLA Modules:
  0.0 94.5 jit_solution(12092214911904625400)
XLA Ops:
  0.0 0.0 copy-start.2
  0.0 1.2 %copy.14 = f32[384,256]{0,1:T(8,128)S(1)} copy(f32[384,256]{1,0:T(8,128)} %param.5) | data formatting | bytes 786432 | tf_op args[1]
  1.2 0.0 copy-done.2
  1.2 0.1 broadcast_in_dim.14
  1.3 0.1 reshape.17
  1.4 3.3 %collective-permute-start = (f32[384,256]{0,1:T(8,128)S(1)}, f32[384,256]{0,1:T(8,128)S(1)}, u32[]{:S(2)}, u32[]{:S(2)}) collective-permute-start(f32[384,256]{0,1:T(8,128)S(1)} %bitcast_multiply_fusion), channel_id=1, source_target_pairs={{0,64},{64,0},{1,65},{65,1},{2,66},{66,2},{3,67},{67,3},{4,68},{68... | collective-permute-start | bytes 1179656 | tf_op jit(solution)/shard_map/ppermute | solution.py:31
  4.7 0.0 copy-done.3
  4.7 0.1 copy.12
  4.8 0.1 broadcast_in_dim.12
  4.8 0.1 reshape.15
  5.0 0.0 copy-start.1
  5.0 0.1 copy.13
  5.1 0.8 copy-done.1
  5.9 2.7 %collective-permute-start.4 = (f32[128,384]{1,0:T(8,128)S(1)}, f32[128,384]{1,0:T(8,128)S(1)}, u32[]{:S(2)}, u32[]{:S(2)}) collective-permute-start(f32[128,384]{1,0:T(8,128)S(1)} %mul.9), channel_id=1, source_target_pairs={{0,128},{8,264},{16,400},{24,24},{32,416},{40,40},{48,176},{56,312... | collective-permute-start | bytes 589832 | tf_op jit(solution)/shard_map/ppermute | solution.py:31
  8.6 8.0 %collective-permute-start.5 = (f32[128,384]{1,0:T(8,128)S(1)}, f32[128,384]{1,0:T(8,128)}, u32[]{:S(2)}, u32[]{:S(2)}) collective-permute-start(f32[128,384]{1,0:T(8,128)S(1)} %mul.9), channel_id=1, source_target_pairs={{0,264},{8,128},{16,24},{24,400},{32,312},{40,176},{48,40},{56,416... | collective-permute-start | bytes 589832 | tf_op jit(solution)/shard_map/ppermute | solution.py:31
  16.6 2.4 %all_gather.7 = f32[384,512]{0,1:T(8,128)S(1)} all-gather(f32[384,256]{0,1:T(8,128)S(1)} %bitcast_multiply_fusion), channel_id=1, replica_groups=mesh['h'=4,'l'=2,'c'=2,'x'=4,'z'=8] {'c'}, dimensions={1}, use_global_device_ids=true | all-gather | bytes 1179648 | tf_op jit(solution)/shard_map/all_gather | solution.py:66
  19.0 2.5 %collective-permute-start.2 = (f32[384,512]{0,1:T(8,128)S(1)}, f32[384,512]{0,1:T(8,128)S(1)}, u32[]{:S(2)}, u32[]{:S(2)}) collective-permute-start(f32[384,512]{0,1:T(8,128)S(1)} %all_gather.7), channel_id=1, source_target_pairs={{0,8},{8,0},{16,24},{24,16},{32,56},{40,48},{48,40},{56,32},{1,9},... | collective-permute-start | bytes 2359304 | tf_op jit(solution)/shard_map/ppermute | solution.py:31
  21.5 0.0 collective-permute-done
  21.5 2.4 %all_gather.6 = f32[384,512]{0,1:T(8,128)S(1)} all-gather(f32[384,256]{0,1:T(8,128)S(1)} %collective-permute-done), channel_id=1, replica_groups=mesh['h'=4,'l'=2,'c'=2,'x'=4,'z'=8] {'c'}, dimensions={1}, use_global_device_ids=true | all-gather | bytes 1179648 | tf_op jit(solution)/shard_map/all_gather | solution.py:74
  23.9 3.3 %collective-permute-start.3 = (f32[384,512]{0,1:T(8,128)S(1)}, f32[384,512]{0,1:T(8,128)S(1)}, u32[]{:S(2)}, u32[]{:S(2)}) collective-permute-start(f32[384,512]{0,1:T(8,128)S(1)} %all_gather.6), channel_id=1, source_target_pairs={{0,8},{8,0},{16,24},{24,16},{32,56},{40,48},{48,40},{56,32},{1,9},... | collective-permute-start | bytes 2359304 | tf_op jit(solution)/shard_map/ppermute | solution.py:31
  27.2 0.0 collective-permute-done.4.own_ref
  27.2 0.0 copy-start.4
  27.2 1.4 %collective-permute-done.5.beside_ref = f32[128,384]{1,0:T(8,128)} collective-permute-done((f32[128,384]{1,0:T(8,128)S(1)}, f32[128,384]{1,0:T(8,128)}, u32[]{:S(2)}, u32[]{:S(2)}) %collective-permute-start.5) | collective-permute-done | bytes 196640 | tf_op jit(solution)/shard_map/ppermute | solution.py:31
  28.6 0.0 copy-done.4
  28.6 1.8 %shard_map.46 = f32[128,768]{1,0:T(8,128)} custom-call(f32[128,384]{1,0:T(8,128)} %copy-done.4, f32[128,384]{1,0:T(8,128)} %collective-permute-done.5.beside_ref), custom_call_target="tpu_custom_call" | custom-call | flops 10000000000 | bytes 1048576 | tf_op jit(solution)/shard_map/pallas_call | solution.py:52
  30.4 2.8 %collective-permute-start.6 = (f32[128,384]{1,0:T(8,128)S(1)}, f32[128,384]{1,0:T(8,128)S(1)}, u32[]{:S(2)}, u32[]{:S(2)}) collective-permute-start(f32[128,384]{1,0:T(8,128)S(1)} %mul.9), channel_id=1, source_target_pairs={{0,392},{8,0},{16,152},{24,272},{32,184},{40,304},{48,424},{56,32}... | collective-permute-start | bytes 589832 | tf_op jit(solution)/shard_map/ppermute | solution.py:31
  33.2 0.7 collective-permute-start.1
  33.9 0.0 collective-permute-done.2
  33.9 1.5 %fusion.3 = f32[128,512]{1,0:T(8,128)S(1)} fusion(f32[384,512]{0,1:T(8,128)S(1)} %collective-permute-done.2, f32[128,768]{1,0:T(8,128)} %shard_map.46), kind=kOutput, calls=%fused_computation.16 | convolution fusion | flops 150994944 | bytes 1245184 | tf_op jit(solution)/shard_map/dot_general | solution.py:40
  35.4 0.0 copy-done
  35.4 0.5 convolution_add_fusion.3
  35.9 7.6 %collective-permute-done.3 = f32[384,512]{0,1:T(8,128)S(1)} collective-permute-done((f32[384,512]{0,1:T(8,128)S(1)}, f32[384,512]{0,1:T(8,128)S(1)}, u32[]{:S(2)}, u32[]{:S(2)}) %collective-permute-start.3) | collective-permute-done | bytes 786464 | tf_op jit(solution)/shard_map/ppermute | solution.py:31
  43.5 0.5 fusion.1
  44.0 0.5 convolution_add_fusion.2
  44.6 1.9 %collective-permute-start.7 = (f32[128,1024]{1,0:T(8,128)S(1)}, f32[128,1024]{1,0:T(8,128)S(1)}, u32[]{:S(2)}, u32[]{:S(2)}) collective-permute-start(f32[128,1024]{1,0:T(8,128)S(1)} %pad_maximum_fusion), channel_id=1, source_target_pairs={{0,24},{8,16},{16,8},{24,0},{32,40},{40,32},{48,56},{56,48},{1,25}... | collective-permute-start | bytes 1572872 | tf_op jit(solution)/shard_map/ppermute | solution.py:31
  46.5 0.0 collective-permute-done.6
  46.5 0.5 fusion.7
  47.1 0.5 fusion.8
  47.6 0.0 collective-permute-done.1
  47.6 0.5 convolution_add_fusion.1
  48.1 0.5 convolution_add_fusion
  48.7 8.2 %collective-permute-done.7 = f32[128,1024]{1,0:T(8,128)S(1)} collective-permute-done((f32[128,1024]{1,0:T(8,128)S(1)}, f32[128,1024]{1,0:T(8,128)S(1)}, u32[]{:S(2)}, u32[]{:S(2)}) %collective-permute-start.7) | collective-permute-done | bytes 524320 | tf_op jit(solution)/shard_map/ppermute | solution.py:31
  56.9 0.1 maximum_add_fusion
  57.1 0.1 fusion
  57.2 23.8 %all_to_all.5 = f32[8,128,128]{2,1,0:T(8,128)S(1)} all-to-all(f32[8,128,128]{2,1,0:T(8,128)S(1)} %fusion), channel_id=1, replica_groups={{0,1,2,3,4,5,6,7},{8,9,10,11,12,13,14,15},{16,17,18,19,20,21,22,23},{24..., dimensions={0} | all-to-all | bytes 1048576 | tf_op jit(solution)/shard_map/all_to_all | solution.py:99
  81.0 3.2 %collective-permute-start.8 = (f32[128,128]{1,0:T(8,128)S(1)}, f32[128,128]{1,0:T(8,128)S(1)}, u32[]{:S(2)}, u32[]{:S(2)}) collective-permute-start(f32[128,128]{1,0:T(8,128)S(1)} %reduce_sum.9), channel_id=1, source_target_pairs={{0,0},{8,128},{16,256},{24,384},{128,136},{136,264},{144,392},{152... | collective-permute-start | bytes 196616 | tf_op jit(solution)/shard_map/ppermute | solution.py:31
  84.3 9.7 %collective-permute-done.8 = f32[128,128]{1,0:T(8,128)S(1)} collective-permute-done((f32[128,128]{1,0:T(8,128)S(1)}, f32[128,128]{1,0:T(8,128)S(1)}, u32[]{:S(2)}, u32[]{:S(2)}) %collective-permute-start.8) | collective-permute-done | bytes 65568 | tf_op jit(solution)/shard_map/ppermute | solution.py:31
  93.9 0.6 copy.19
  (12 shorter events, 0.2 us)
Async XLA Ops:
  0.0 1.2 %copy-start.2 = (s32[6,4]{0,1:T(4,128)S(1)}, s32[6,4]{0,1:T(4,128)}, u32[]{:S(2)}) copy-start(s32[6,4]{0,1:T(4,128)} %param.7) | copy-start | bytes 292
  1.4 3.3 %copy-start.3 = (s32[2,6]{1,0:T(2,128)S(1)}, s32[2,6]{1,0:T(2,128)}, u32[]{:S(2)}) copy-start(s32[2,6]{1,0:T(2,128)} %param.6) | copy-start | bytes 148
  1.4 20.1 %collective-permute-start = (f32[384,256]{0,1:T(8,128)S(1)}, f32[384,256]{0,1:T(8,128)S(1)}, u32[]{:S(2)}, u32[]{:S(2)}) collective-permute-start(f32[384,256]{0,1:T(8,128)S(1)} %bitcast_multiply_fusion), channel_id=1, source_target_pairs={{0,64},{64,0},{1,65},{65,1},{2,66},{66,2},{3,67},{67,3},{4,68},{68... | collective-permute-start | bytes 1179656 | tf_op jit(solution)/shard_map/ppermute | solution.py:31
  5.0 0.9 copy-start.1
  5.9 21.3 %collective-permute-start.4 = (f32[128,384]{1,0:T(8,128)S(1)}, f32[128,384]{1,0:T(8,128)S(1)}, u32[]{:S(2)}, u32[]{:S(2)}) collective-permute-start(f32[128,384]{1,0:T(8,128)S(1)} %mul.9), channel_id=1, source_target_pairs={{0,128},{8,264},{16,400},{24,24},{32,416},{40,40},{48,176},{56,312... | collective-permute-start | bytes 589832 | tf_op jit(solution)/shard_map/ppermute | solution.py:31
  8.6 20.0 %collective-permute-start.5 = (f32[128,384]{1,0:T(8,128)S(1)}, f32[128,384]{1,0:T(8,128)}, u32[]{:S(2)}, u32[]{:S(2)}) collective-permute-start(f32[128,384]{1,0:T(8,128)S(1)} %mul.9), channel_id=1, source_target_pairs={{0,264},{8,128},{16,24},{24,400},{32,312},{40,176},{48,40},{56,416... | collective-permute-start | bytes 589832 | tf_op jit(solution)/shard_map/ppermute | solution.py:31
  19.0 14.9 %collective-permute-start.2 = (f32[384,512]{0,1:T(8,128)S(1)}, f32[384,512]{0,1:T(8,128)S(1)}, u32[]{:S(2)}, u32[]{:S(2)}) collective-permute-start(f32[384,512]{0,1:T(8,128)S(1)} %all_gather.7), channel_id=1, source_target_pairs={{0,8},{8,0},{16,24},{24,16},{32,56},{40,48},{48,40},{56,32},{1,9},... | collective-permute-start | bytes 2359304 | tf_op jit(solution)/shard_map/ppermute | solution.py:31
  23.9 19.6 %collective-permute-start.3 = (f32[384,512]{0,1:T(8,128)S(1)}, f32[384,512]{0,1:T(8,128)S(1)}, u32[]{:S(2)}, u32[]{:S(2)}) collective-permute-start(f32[384,512]{0,1:T(8,128)S(1)} %all_gather.6), channel_id=1, source_target_pairs={{0,8},{8,0},{16,24},{24,16},{32,56},{40,48},{48,40},{56,32},{1,9},... | collective-permute-start | bytes 2359304 | tf_op jit(solution)/shard_map/ppermute | solution.py:31
  27.2 1.4 %copy-start.4 = (f32[128,384]{1,0:T(8,128)}, f32[128,384]{1,0:T(8,128)S(1)}, u32[]{:S(2)}) copy-start(f32[128,384]{1,0:T(8,128)S(1)} %collective-permute-done.4.own_ref) | copy-start | bytes 589828
  30.4 5.0 %copy-start = (f32[128,768]{1,0:T(8,128)S(1)}, f32[128,768]{1,0:T(8,128)}, u32[]{:S(2)}) copy-start(f32[128,768]{1,0:T(8,128)} %shard_map.46) | copy-start | bytes 1179652
  30.4 16.1 %collective-permute-start.6 = (f32[128,384]{1,0:T(8,128)S(1)}, f32[128,384]{1,0:T(8,128)S(1)}, u32[]{:S(2)}, u32[]{:S(2)}) collective-permute-start(f32[128,384]{1,0:T(8,128)S(1)} %mul.9), channel_id=1, source_target_pairs={{0,392},{8,0},{16,152},{24,272},{32,184},{40,304},{48,424},{56,32}... | collective-permute-start | bytes 589832 | tf_op jit(solution)/shard_map/ppermute | solution.py:31
  33.2 14.4 %collective-permute-start.1 = (f32[128,384]{1,0:T(8,128)S(1)}, f32[128,384]{1,0:T(8,128)S(1)}, u32[]{:S(2)}, u32[]{:S(2)}) collective-permute-start(f32[128,384]{1,0:T(8,128)S(1)} %mul.9), channel_id=1, source_target_pairs={{0,0},{8,392},{16,272},{24,152},{32,32},{40,424},{48,304},{56,184}... | collective-permute-start | bytes 589832 | tf_op jit(solution)/shard_map/ppermute | solution.py:31
  44.6 12.3 %collective-permute-start.7 = (f32[128,1024]{1,0:T(8,128)S(1)}, f32[128,1024]{1,0:T(8,128)S(1)}, u32[]{:S(2)}, u32[]{:S(2)}) collective-permute-start(f32[128,1024]{1,0:T(8,128)S(1)} %pad_maximum_fusion), channel_id=1, source_target_pairs={{0,24},{8,16},{16,8},{24,0},{32,40},{40,32},{48,56},{56,48},{1,25}... | collective-permute-start | bytes 1572872 | tf_op jit(solution)/shard_map/ppermute | solution.py:31
  81.0 12.9 %collective-permute-start.8 = (f32[128,128]{1,0:T(8,128)S(1)}, f32[128,128]{1,0:T(8,128)S(1)}, u32[]{:S(2)}, u32[]{:S(2)}) collective-permute-start(f32[128,128]{1,0:T(8,128)S(1)} %reduce_sum.9), channel_id=1, source_target_pairs={{0,0},{8,128},{16,256},{24,384},{128,136},{136,264},{144,392},{152... | collective-permute-start | bytes 196616 | tf_op jit(solution)/shard_map/ppermute | solution.py:31

commit v5 on v4

--- a/solution.py
+++ b/solution.py
@@ -58,6 +58,10 @@
     )(own, beside)
 
 
+def ahead(at):
+    return at["x"] + 2 * at["l"]
+
+
 def body(amplitudes, integrals, pair_mask, tile_mask):
     l = lax.axis_index("l")
     width = amplitudes.shape[1] // pair_mask.shape[1]
@@ -66,15 +70,15 @@
     near = lax.all_gather(masked_v, "c", axis=1, tiled=True)
     near_beside = send(near, ("c", "x"), lambda at: {"x": at["x"] + sign(at)})
     masked_t = amplitudes * expand(pair_mask, width)
-    names = ("h", "c", "x")
-    own_b = send(masked_t, names, lambda at: {"h": at["h"] - at["x"] + sign(at)})
-    beside_b = send(masked_t, names, lambda at: {"h": at["h"] - at["x"] - 2 * sign(at), "x": at["x"] + sign(at)})
+    names = ("h", "l", "c", "x")
+    own_b = send(masked_t, names, lambda at: {"h": at["h"] - ahead(at) + sign(at)})
+    beside_b = send(masked_t, names, lambda at: {"h": at["h"] - ahead(at) - 2 * sign(at), "x": at["x"] + sign(at)})
     staged = stage_rows(own_b, beside_b)
     own_b, beside_b = staged[:, :384], staged[:, 384:]
     far = lax.all_gather(far_half, "c", axis=1, tiled=True)
     masked_t, far = lax.optimization_barrier((masked_t, far))
-    own_a = send(masked_t, names, lambda at: {"h": at["h"] - at["x"]})
-    beside_a = send(masked_t, names, lambda at: {"h": at["h"] - at["x"] - sign(at), "x": at["x"] + sign(at)})
+    own_a = send(masked_t, names, lambda at: {"h": at["h"] - ahead(at)})
+    beside_a = send(masked_t, names, lambda at: {"h": at["h"] - ahead(at) - sign(at), "x": at["x"] + sign(at)})
     far_beside = send(far, ("c", "x"), lambda at: {"x": at["x"] + sign(at)})
     def block(own, beside, near, near_beside, far, far_beside):
         near_block = product(own, near) + product(beside, near_beside)
@@ -97,7 +101,7 @@
     pieces = jnp.concatenate([pieces, pieces[:4]])
     pieces = lax.dynamic_slice_in_dim(pieces, turn, 8, 0)
     total = lax.all_to_all(pieces, AXES, 0, 0, tiled=True, axis_index_groups=groups).sum(0)
-    return send(total, ("h", "x"), lambda at: {"h": at["h"] + at["x"], "x": at["h"]})
+    return send(total, ("h", "l", "x"), lambda at: {"h": at["h"] + ahead(at), "x": at["h"]})
 
 
 def solution(mesh):

time: 95 us -> 93.9 us (0.988)
  the two profiles are of different devices: /device:TPU:40 before, /device:TPU:30 now
where the time goes in v5:
time: 93.9 us; the launch traced here: 93.5 us
  starting transfers between devices  30.4 us (32%)
  blocking collectives  28.1 us (30%)
  waiting for transfers between devices  24.2 us (26%)
  matrix products  5.14 us (5%)
  local copies, waits for them, and re-layouts  3.17 us (3%)
  Pallas kernels  1.79 us (2%)
    ppermute x9, starting transfers between devices, send(): return lax.ppermute(value, names, moves(names, target))  30.4 us
    ppermute x9, waiting for transfers between devices, send(): return lax.ppermute(value, names, moves(names, target))  24.2 us
    all_to_all x1, blocking collectives, body(): lax.all_to_all(pieces, AXES, 0, 0, tiled=True, axis_index_groups=groups)  23.4 us
    dot_general x8, matrix products, product(): jnp.dot(a, b, precision=lax.Precision.HIGH, preferred_element_type=jnp.fl...  5.14 us
    unnamed x12, local copies, waits for them, and re-layouts  2.61 us
    all_gather x1, blocking collectives, body(): near = lax.all_gather(masked_v, 'c', axis=1, tiled=True)  2.37 us
    all_gather x1, blocking collectives, body(): far = lax.all_gather(far_half, 'c', axis=1, tiled=True)  2.36 us
  transfers between devices with their start and end apart: 9, of which 5 were waited for; matrix products, arithmetic and copies ran while one was open for 6% of the time, Pallas kernels for 2%

profile of v5, /device:TPU:30, one launch (start us, length us, event | category | flops | bytes accessed | tf_op | source)
XLA Modules:
  0.0 93.5 jit_solution(13309042469015678435)
XLA Ops:
  0.0 0.0 copy-start.2
  0.0 1.2 %copy.14 = f32[384,256]{0,1:T(8,128)S(1)} copy(f32[384,256]{1,0:T(8,128)} %param.5) | data formatting | bytes 786432 | tf_op args[1]
  1.2 0.0 copy-done.2
  1.2 0.1 broadcast_in_dim.14
  1.3 0.1 reshape.17
  1.4 2.4 %collective-permute-start = (f32[384,256]{0,1:T(8,128)S(1)}, f32[384,256]{0,1:T(8,128)S(1)}, u32[]{:S(2)}, u32[]{:S(2)}) collective-permute-start(f32[384,256]{0,1:T(8,128)S(1)} %bitcast_multiply_fusion), channel_id=1, source_target_pairs={{0,64},{64,0},{1,65},{65,1},{2,66},{66,2},{3,67},{67,3},{4,68},{68... | collective-permute-start | bytes 1179656 | tf_op jit(solution)/shard_map/ppermute | solution.py:31
  3.8 0.0 copy-done.3
  3.8 0.1 copy.12
  3.9 0.1 broadcast_in_dim.12
  3.9 0.1 reshape.15
  4.1 0.0 copy-start.1
  4.1 0.1 copy.13
  4.2 0.8 copy-done.1
  5.0 5.9 %collective-permute-start.4 = (f32[128,384]{1,0:T(8,128)S(1)}, f32[128,384]{1,0:T(8,128)S(1)}, u32[]{:S(2)}, u32[]{:S(2)}) collective-permute-start(f32[128,384]{1,0:T(8,128)S(1)} %mul.9), channel_id=1, source_target_pairs={{0,128},{8,264},{16,400},{24,24},{32,416},{40,40},{48,176},{56,312... | collective-permute-start | bytes 589832 | tf_op jit(solution)/shard_map/ppermute | solution.py:31
  10.9 2.7 %collective-permute-start.5 = (f32[128,384]{1,0:T(8,128)S(1)}, f32[128,384]{1,0:T(8,128)}, u32[]{:S(2)}, u32[]{:S(2)}) collective-permute-start(f32[128,384]{1,0:T(8,128)S(1)} %mul.9), channel_id=1, source_target_pairs={{0,264},{8,128},{16,24},{24,400},{32,312},{40,176},{48,40},{56,416... | collective-permute-start | bytes 589832 | tf_op jit(solution)/shard_map/ppermute | solution.py:31
  13.7 2.4 %all_gather.7 = f32[384,512]{0,1:T(8,128)S(1)} all-gather(f32[384,256]{0,1:T(8,128)S(1)} %bitcast_multiply_fusion), channel_id=1, replica_groups=mesh['h'=4,'l'=2,'c'=2,'x'=4,'z'=8] {'c'}, dimensions={1}, use_global_device_ids=true | all-gather | bytes 1179648 | tf_op jit(solution)/shard_map/all_gather | solution.py:70
  16.1 4.4 %collective-permute-start.2 = (f32[384,512]{0,1:T(8,128)S(1)}, f32[384,512]{0,1:T(8,128)S(1)}, u32[]{:S(2)}, u32[]{:S(2)}) collective-permute-start(f32[384,512]{0,1:T(8,128)S(1)} %all_gather.7), channel_id=1, source_target_pairs={{0,8},{8,0},{16,24},{24,16},{32,56},{40,48},{48,40},{56,32},{1,9},... | collective-permute-start | bytes 2359304 | tf_op jit(solution)/shard_map/ppermute | solution.py:31
  20.5 1.1 %collective-permute-done = f32[384,256]{0,1:T(8,128)S(1)} collective-permute-done((f32[384,256]{0,1:T(8,128)S(1)}, f32[384,256]{0,1:T(8,128)S(1)}, u32[]{:S(2)}, u32[]{:S(2)}) %collective-permute-start) | collective-permute-done | bytes 393248 | tf_op jit(solution)/shard_map/ppermute | solution.py:31
  21.6 2.4 %all_gather.6 = f32[384,512]{0,1:T(8,128)S(1)} all-gather(f32[384,256]{0,1:T(8,128)S(1)} %collective-permute-done), channel_id=1, replica_groups=mesh['h'=4,'l'=2,'c'=2,'x'=4,'z'=8] {'c'}, dimensions={1}, use_global_device_ids=true | all-gather | bytes 1179648 | tf_op jit(solution)/shard_map/all_gather | solution.py:78
  24.0 1.9 %collective-permute-start.3 = (f32[384,512]{0,1:T(8,128)S(1)}, f32[384,512]{0,1:T(8,128)S(1)}, u32[]{:S(2)}, u32[]{:S(2)}) collective-permute-start(f32[384,512]{0,1:T(8,128)S(1)} %all_gather.6), channel_id=1, source_target_pairs={{0,8},{8,0},{16,24},{24,16},{32,56},{40,48},{48,40},{56,32},{1,9},... | collective-permute-start | bytes 2359304 | tf_op jit(solution)/shard_map/ppermute | solution.py:31
  25.9 0.0 collective-permute-done.4.own_ref
  25.9 0.0 copy-start.4
  25.9 3.2 %collective-permute-done.5.beside_ref = f32[128,384]{1,0:T(8,128)} collective-permute-done((f32[128,384]{1,0:T(8,128)S(1)}, f32[128,384]{1,0:T(8,128)}, u32[]{:S(2)}, u32[]{:S(2)}) %collective-permute-start.5) | collective-permute-done | bytes 196640 | tf_op jit(solution)/shard_map/ppermute | solution.py:31
  29.1 0.0 copy-done.4
  29.1 1.8 %shard_map.46 = f32[128,768]{1,0:T(8,128)} custom-call(f32[128,384]{1,0:T(8,128)} %copy-done.4, f32[128,384]{1,0:T(8,128)} %collective-permute-done.5.beside_ref), custom_call_target="tpu_custom_call" | custom-call | flops 10000000000 | bytes 1048576 | tf_op jit(solution)/shard_map/pallas_call | solution.py:52
  30.9 2.0 %collective-permute-start.6 = (f32[128,384]{1,0:T(8,128)S(1)}, f32[128,384]{1,0:T(8,128)S(1)}, u32[]{:S(2)}, u32[]{:S(2)}) collective-permute-start(f32[128,384]{1,0:T(8,128)S(1)} %mul.9), channel_id=1, source_target_pairs={{0,392},{8,0},{16,152},{24,272},{32,184},{40,304},{48,424},{56,32}... | collective-permute-start | bytes 589832 | tf_op jit(solution)/shard_map/ppermute | solution.py:31
  33.0 3.2 %collective-permute-start.1 = (f32[128,384]{1,0:T(8,128)S(1)}, f32[128,384]{1,0:T(8,128)S(1)}, u32[]{:S(2)}, u32[]{:S(2)}) collective-permute-start(f32[128,384]{1,0:T(8,128)S(1)} %mul.9), channel_id=1, source_target_pairs={{0,0},{8,392},{16,272},{24,152},{32,32},{40,424},{48,304},{56,184}... | collective-permute-start | bytes 589832 | tf_op jit(solution)/shard_map/ppermute | solution.py:31
  36.1 0.0 collective-permute-done.2
  36.2 1.5 %fusion.3 = f32[128,512]{1,0:T(8,128)S(1)} fusion(f32[384,512]{0,1:T(8,128)S(1)} %collective-permute-done.2, f32[128,768]{1,0:T(8,128)} %shard_map.46), kind=kOutput, calls=%fused_computation.16 | convolution fusion | flops 150994944 | bytes 1245184 | tf_op jit(solution)/shard_map/dot_general | solution.py:40
  37.6 0.0 copy-done
  37.6 0.5 convolution_add_fusion.3
  38.2 5.0 %collective-permute-done.3 = f32[384,512]{0,1:T(8,128)S(1)} collective-permute-done((f32[384,512]{0,1:T(8,128)S(1)}, f32[384,512]{0,1:T(8,128)S(1)}, u32[]{:S(2)}, u32[]{:S(2)}) %collective-permute-start.3) | collective-permute-done | bytes 786464 | tf_op jit(solution)/shard_map/ppermute | solution.py:31
  43.1 0.5 fusion.1
  43.6 0.5 convolution_add_fusion.2
  44.2 2.4 %collective-permute-start.7 = (f32[128,1024]{1,0:T(8,128)S(1)}, f32[128,1024]{1,0:T(8,128)S(1)}, u32[]{:S(2)}, u32[]{:S(2)}) collective-permute-start(f32[128,1024]{1,0:T(8,128)S(1)} %pad_maximum_fusion), channel_id=1, source_target_pairs={{0,24},{8,16},{16,8},{24,0},{32,40},{40,32},{48,56},{56,48},{1,25}... | collective-permute-start | bytes 1572872 | tf_op jit(solution)/shard_map/ppermute | solution.py:31
  46.6 0.0 collective-permute-done.6
  46.6 0.5 fusion.7
  47.1 0.5 fusion.8
  47.7 0.0 collective-permute-done.1
  47.7 0.5 convolution_add_fusion.1
  48.2 0.5 convolution_add_fusion
  48.7 7.8 %collective-permute-done.7 = f32[128,1024]{1,0:T(8,128)S(1)} collective-permute-done((f32[128,1024]{1,0:T(8,128)S(1)}, f32[128,1024]{1,0:T(8,128)S(1)}, u32[]{:S(2)}, u32[]{:S(2)}) %collective-permute-start.7) | collective-permute-done | bytes 524320 | tf_op jit(solution)/shard_map/ppermute | solution.py:31
  56.5 0.1 maximum_add_fusion
  56.7 0.1 fusion
  56.8 23.4 %all_to_all.5 = f32[8,128,128]{2,1,0:T(8,128)S(1)} all-to-all(f32[8,128,128]{2,1,0:T(8,128)S(1)} %fusion), channel_id=1, replica_groups={{0,1,2,3,4,5,6,7},{8,9,10,11,12,13,14,15},{16,17,18,19,20,21,22,23},{24..., dimensions={0} | all-to-all | bytes 1048576 | tf_op jit(solution)/shard_map/all_to_all | solution.py:103
  80.2 5.5 %collective-permute-start.8 = (f32[128,128]{1,0:T(8,128)S(1)}, f32[128,128]{1,0:T(8,128)S(1)}, u32[]{:S(2)}, u32[]{:S(2)}) collective-permute-start(f32[128,128]{1,0:T(8,128)S(1)} %reduce_sum.9), channel_id=1, source_target_pairs={{0,0},{8,128},{16,256},{24,384},{64,320},{72,448},{80,64},{88,192}... | collective-permute-start | bytes 196616 | tf_op jit(solution)/shard_map/ppermute | solution.py:31
  85.7 7.1 %collective-permute-done.8 = f32[128,128]{1,0:T(8,128)S(1)} collective-permute-done((f32[128,128]{1,0:T(8,128)S(1)}, f32[128,128]{1,0:T(8,128)S(1)}, u32[]{:S(2)}, u32[]{:S(2)}) %collective-permute-start.8) | collective-permute-done | bytes 65568 | tf_op jit(solution)/shard_map/ppermute | solution.py:31
  92.9 0.6 copy.19
  (12 shorter events, 0.2 us)
Async XLA Ops:
  0.0 1.2 %copy-start.2 = (s32[6,4]{0,1:T(4,128)S(1)}, s32[6,4]{0,1:T(4,128)}, u32[]{:S(2)}) copy-start(s32[6,4]{0,1:T(4,128)} %param.7) | copy-start | bytes 292
  1.4 2.4 %copy-start.3 = (s32[2,6]{1,0:T(2,128)S(1)}, s32[2,6]{1,0:T(2,128)}, u32[]{:S(2)}) copy-start(s32[2,6]{1,0:T(2,128)} %param.6) | copy-start | bytes 148
  1.4 20.2 %collective-permute-start = (f32[384,256]{0,1:T(8,128)S(1)}, f32[384,256]{0,1:T(8,128)S(1)}, u32[]{:S(2)}, u32[]{:S(2)}) collective-permute-start(f32[384,256]{0,1:T(8,128)S(1)} %bitcast_multiply_fusion), channel_id=1, source_target_pairs={{0,64},{64,0},{1,65},{65,1},{2,66},{66,2},{3,67},{67,3},{4,68},{68... | collective-permute-start | bytes 1179656 | tf_op jit(solution)/shard_map/ppermute | solution.py:31
  4.1 0.9 copy-start.1
  5.0 20.9 %collective-permute-start.4 = (f32[128,384]{1,0:T(8,128)S(1)}, f32[128,384]{1,0:T(8,128)S(1)}, u32[]{:S(2)}, u32[]{:S(2)}) collective-permute-start(f32[128,384]{1,0:T(8,128)S(1)} %mul.9), channel_id=1, source_target_pairs={{0,128},{8,264},{16,400},{24,24},{32,416},{40,40},{48,176},{56,312... | collective-permute-start | bytes 589832 | tf_op jit(solution)/shard_map/ppermute | solution.py:31
  10.9 18.2 %collective-permute-start.5 = (f32[128,384]{1,0:T(8,128)S(1)}, f32[128,384]{1,0:T(8,128)}, u32[]{:S(2)}, u32[]{:S(2)}) collective-permute-start(f32[128,384]{1,0:T(8,128)S(1)} %mul.9), channel_id=1, source_target_pairs={{0,264},{8,128},{16,24},{24,400},{32,312},{40,176},{48,40},{56,416... | collective-permute-start | bytes 589832 | tf_op jit(solution)/shard_map/ppermute | solution.py:31
  16.1 20.1 %collective-permute-start.2 = (f32[384,512]{0,1:T(8,128)S(1)}, f32[384,512]{0,1:T(8,128)S(1)}, u32[]{:S(2)}, u32[]{:S(2)}) collective-permute-start(f32[384,512]{0,1:T(8,128)S(1)} %all_gather.7), channel_id=1, source_target_pairs={{0,8},{8,0},{16,24},{24,16},{32,56},{40,48},{48,40},{56,32},{1,9},... | collective-permute-start | bytes 2359304 | tf_op jit(solution)/shard_map/ppermute | solution.py:31
  24.0 19.1 %collective-permute-start.3 = (f32[384,512]{0,1:T(8,128)S(1)}, f32[384,512]{0,1:T(8,128)S(1)}, u32[]{:S(2)}, u32[]{:S(2)}) collective-permute-start(f32[384,512]{0,1:T(8,128)S(1)} %all_gather.6), channel_id=1, source_target_pairs={{0,8},{8,0},{16,24},{24,16},{32,56},{40,48},{48,40},{56,32},{1,9},... | collective-permute-start | bytes 2359304 | tf_op jit(solution)/shard_map/ppermute | solution.py:31
  25.9 3.2 %copy-start.4 = (f32[128,384]{1,0:T(8,128)}, f32[128,384]{1,0:T(8,128)S(1)}, u32[]{:S(2)}) copy-start(f32[128,384]{1,0:T(8,128)S(1)} %collective-permute-done.4.own_ref) | copy-start | bytes 589828
  30.9 6.7 %copy-start = (f32[128,768]{1,0:T(8,128)S(1)}, f32[128,768]{1,0:T(8,128)}, u32[]{:S(2)}) copy-start(f32[128,768]{1,0:T(8,128)} %shard_map.46) | copy-start | bytes 1179652
  30.9 15.7 %collective-permute-start.6 = (f32[128,384]{1,0:T(8,128)S(1)}, f32[128,384]{1,0:T(8,128)S(1)}, u32[]{:S(2)}, u32[]{:S(2)}) collective-permute-start(f32[128,384]{1,0:T(8,128)S(1)} %mul.9), channel_id=1, source_target_pairs={{0,392},{8,0},{16,152},{24,272},{32,184},{40,304},{48,424},{56,32}... | collective-permute-start | bytes 589832 | tf_op jit(solution)/shard_map/ppermute | solution.py:31
  33.0 14.7 %collective-permute-start.1 = (f32[128,384]{1,0:T(8,128)S(1)}, f32[128,384]{1,0:T(8,128)S(1)}, u32[]{:S(2)}, u32[]{:S(2)}) collective-permute-start(f32[128,384]{1,0:T(8,128)S(1)} %mul.9), channel_id=1, source_target_pairs={{0,0},{8,392},{16,272},{24,152},{32,32},{40,424},{48,304},{56,184}... | collective-permute-start | bytes 589832 | tf_op jit(solution)/shard_map/ppermute | solution.py:31
  44.2 12.3 %collective-permute-start.7 = (f32[128,1024]{1,0:T(8,128)S(1)}, f32[128,1024]{1,0:T(8,128)S(1)}, u32[]{:S(2)}, u32[]{:S(2)}) collective-permute-start(f32[128,1024]{1,0:T(8,128)S(1)} %pad_maximum_fusion), channel_id=1, source_target_pairs={{0,24},{8,16},{16,8},{24,0},{32,40},{40,32},{48,56},{56,48},{1,25}... | collective-permute-start | bytes 1572872 | tf_op jit(solution)/shard_map/ppermute | solution.py:31
  80.2 12.6 %collective-permute-start.8 = (f32[128,128]{1,0:T(8,128)S(1)}, f32[128,128]{1,0:T(8,128)S(1)}, u32[]{:S(2)}, u32[]{:S(2)}) collective-permute-start(f32[128,128]{1,0:T(8,128)S(1)} %reduce_sum.9), channel_id=1, source_target_pairs={{0,0},{8,128},{16,256},{24,384},{64,320},{72,448},{80,64},{88,192}... | collective-permute-start | bytes 196616 | tf_op jit(solution)/shard_map/ppermute | solution.py:31

commit v6 on v5

--- a/solution.py
+++ b/solution.py
@@ -59,7 +59,7 @@
 
 
 def ahead(at):
-    return at["x"] + 2 * at["l"]
+    return at["x"] + 2 * at["l"] + 1
 
 
 def body(amplitudes, integrals, pair_mask, tile_mask):

time: 93.9 us -> 93.8 us (level)
  the two profiles are of different devices: /device:TPU:30 before, /device:TPU:40 now
where the time goes in v6:
time: 93.8 us; the launch traced here: 93.4 us
  starting transfers between devices  30.1 us (32%)
  blocking collectives  27.5 us (29%)
  waiting for transfers between devices  25.1 us (27%)
  matrix products  5.15 us (5%)
  local copies, waits for them, and re-layouts  3.17 us (3%)
  Pallas kernels  1.79 us (2%)
    ppermute x9, starting transfers between devices, send(): return lax.ppermute(value, names, moves(names, target))  30.1 us
    ppermute x9, waiting for transfers between devices, send(): return lax.ppermute(value, names, moves(names, target))  25.1 us
    all_to_all x1, blocking collectives, body(): lax.all_to_all(pieces, AXES, 0, 0, tiled=True, axis_index_groups=groups)  22.7 us
    dot_general x8, matrix products, product(): jnp.dot(a, b, precision=lax.Precision.HIGH, preferred_element_type=jnp.fl...  5.15 us
    unnamed x12, local copies, waits for them, and re-layouts  2.61 us
    all_gather x1, blocking collectives, body(): near = lax.all_gather(masked_v, 'c', axis=1, tiled=True)  2.37 us
    all_gather x1, blocking collectives, body(): far = lax.all_gather(far_half, 'c', axis=1, tiled=True)  2.37 us
  transfers between devices with their start and end apart: 9, of which 4 were waited for; matrix products, arithmetic and copies ran while one was open for 6% of the time, Pallas kernels for 2%

profile of v6, /device:TPU:40, one launch (start us, length us, event | category | flops | bytes accessed | tf_op | source)
XLA Modules:
  0.0 93.4 jit_solution(12084052976275158325)
XLA Ops:
  0.0 0.0 copy-start.2
  0.0 1.2 %copy.14 = f32[384,256]{0,1:T(8,128)S(1)} copy(f32[384,256]{1,0:T(8,128)} %param.5) | data formatting | bytes 786432 | tf_op args[1]
  1.2 0.0 copy-done.2
  1.2 0.1 broadcast_in_dim.14
  1.3 0.1 reshape.17
  1.4 3.3 %collective-permute-start = (f32[384,256]{0,1:T(8,128)S(1)}, f32[384,256]{0,1:T(8,128)S(1)}, u32[]{:S(2)}, u32[]{:S(2)}) collective-permute-start(f32[384,256]{0,1:T(8,128)S(1)} %bitcast_multiply_fusion), channel_id=1, source_target_pairs={{0,64},{64,0},{1,65},{65,1},{2,66},{66,2},{3,67},{67,3},{4,68},{68... | collective-permute-start | bytes 1179656 | tf_op jit(solution)/shard_map/ppermute | solution.py:31
  4.7 0.0 copy-done.3
  4.7 0.1 copy.12
  4.8 0.1 broadcast_in_dim.12
  4.8 0.1 reshape.15
  5.0 0.0 copy-start.1
  5.0 0.1 copy.13
  5.1 0.8 copy-done.1
  5.9 7.4 %collective-permute-start.4 = (f32[128,384]{1,0:T(8,128)S(1)}, f32[128,384]{1,0:T(8,128)S(1)}, u32[]{:S(2)}, u32[]{:S(2)}) collective-permute-start(f32[128,384]{1,0:T(8,128)S(1)} %mul.9), channel_id=1, source_target_pairs={{0,0},{8,136},{16,272},{24,408},{32,288},{40,424},{48,48},{56,184}... | collective-permute-start | bytes 589832 | tf_op jit(solution)/shard_map/ppermute | solution.py:31
  13.3 1.9 %collective-permute-start.5 = (f32[128,384]{1,0:T(8,128)S(1)}, f32[128,384]{1,0:T(8,128)}, u32[]{:S(2)}, u32[]{:S(2)}) collective-permute-start(f32[128,384]{1,0:T(8,128)S(1)} %mul.9), channel_id=1, source_target_pairs={{0,136},{8,0},{16,408},{24,272},{32,184},{40,48},{48,424},{56,288}... | collective-permute-start | bytes 589832 | tf_op jit(solution)/shard_map/ppermute | solution.py:31
  15.2 2.4 %all_gather.7 = f32[384,512]{0,1:T(8,128)S(1)} all-gather(f32[384,256]{0,1:T(8,128)S(1)} %bitcast_multiply_fusion), channel_id=1, replica_groups=mesh['h'=4,'l'=2,'c'=2,'x'=4,'z'=8] {'c'}, dimensions={1}, use_global_device_ids=true | all-gather | bytes 1179648 | tf_op jit(solution)/shard_map/all_gather | solution.py:70
  17.6 3.8 %collective-permute-start.2 = (f32[384,512]{0,1:T(8,128)S(1)}, f32[384,512]{0,1:T(8,128)S(1)}, u32[]{:S(2)}, u32[]{:S(2)}) collective-permute-start(f32[384,512]{0,1:T(8,128)S(1)} %all_gather.7), channel_id=1, source_target_pairs={{0,8},{8,0},{16,24},{24,16},{32,56},{40,48},{48,40},{56,32},{1,9},... | collective-permute-start | bytes 2359304 | tf_op jit(solution)/shard_map/ppermute | solution.py:31
  21.4 0.0 collective-permute-done
  21.4 2.4 %all_gather.6 = f32[384,512]{0,1:T(8,128)S(1)} all-gather(f32[384,256]{0,1:T(8,128)S(1)} %collective-permute-done), channel_id=1, replica_groups=mesh['h'=4,'l'=2,'c'=2,'x'=4,'z'=8] {'c'}, dimensions={1}, use_global_device_ids=true | all-gather | bytes 1179648 | tf_op jit(solution)/shard_map/all_gather | solution.py:78
  23.8 2.0 %collective-permute-start.3 = (f32[384,512]{0,1:T(8,128)S(1)}, f32[384,512]{0,1:T(8,128)S(1)}, u32[]{:S(2)}, u32[]{:S(2)}) collective-permute-start(f32[384,512]{0,1:T(8,128)S(1)} %all_gather.6), channel_id=1, source_target_pairs={{0,8},{8,0},{16,24},{24,16},{32,56},{40,48},{48,40},{56,32},{1,9},... | collective-permute-start | bytes 2359304 | tf_op jit(solution)/shard_map/ppermute | solution.py:31
  25.8 0.0 collective-permute-done.4.own_ref
  25.8 0.0 copy-start.4
  25.8 1.7 %collective-permute-done.5.beside_ref = f32[128,384]{1,0:T(8,128)} collective-permute-done((f32[128,384]{1,0:T(8,128)S(1)}, f32[128,384]{1,0:T(8,128)}, u32[]{:S(2)}, u32[]{:S(2)}) %collective-permute-start.5) | collective-permute-done | bytes 196640 | tf_op jit(solution)/shard_map/ppermute | solution.py:31
  27.5 0.0 copy-done.4
  27.6 1.8 %shard_map.46 = f32[128,768]{1,0:T(8,128)} custom-call(f32[128,384]{1,0:T(8,128)} %copy-done.4, f32[128,384]{1,0:T(8,128)} %collective-permute-done.5.beside_ref), custom_call_target="tpu_custom_call" | custom-call | flops 10000000000 | bytes 1048576 | tf_op jit(solution)/shard_map/pallas_call | solution.py:52
  29.3 2.9 %collective-permute-start.6 = (f32[128,384]{1,0:T(8,128)S(1)}, f32[128,384]{1,0:T(8,128)S(1)}, u32[]{:S(2)}, u32[]{:S(2)}) collective-permute-start(f32[128,384]{1,0:T(8,128)S(1)} %mul.9), channel_id=1, source_target_pairs={{0,264},{8,384},{16,24},{24,144},{32,56},{40,176},{48,296},{56,416... | collective-permute-start | bytes 589832 | tf_op jit(solution)/shard_map/ppermute | solution.py:31
  32.2 2.7 %collective-permute-start.1 = (f32[128,384]{1,0:T(8,128)S(1)}, f32[128,384]{1,0:T(8,128)S(1)}, u32[]{:S(2)}, u32[]{:S(2)}) collective-permute-start(f32[128,384]{1,0:T(8,128)S(1)} %mul.9), channel_id=1, source_target_pairs={{0,384},{8,264},{16,144},{24,24},{32,416},{40,296},{48,176},{56,56... | collective-permute-start | bytes 589832 | tf_op jit(solution)/shard_map/ppermute | solution.py:31
  34.9 0.0 collective-permute-done.2
  35.0 1.5 %fusion.3 = f32[128,512]{1,0:T(8,128)S(1)} fusion(f32[384,512]{0,1:T(8,128)S(1)} %collective-permute-done.2, f32[128,768]{1,0:T(8,128)} %shard_map.46), kind=kOutput, calls=%fused_computation.16 | convolution fusion | flops 150994944 | bytes 1245184 | tf_op jit(solution)/shard_map/dot_general | solution.py:40
  36.4 0.0 copy-done
  36.4 0.5 convolution_add_fusion.3
  37.0 7.2 %collective-permute-done.3 = f32[384,512]{0,1:T(8,128)S(1)} collective-permute-done((f32[384,512]{0,1:T(8,128)S(1)}, f32[384,512]{0,1:T(8,128)S(1)}, u32[]{:S(2)}, u32[]{:S(2)}) %collective-permute-start.3) | collective-permute-done | bytes 786464 | tf_op jit(solution)/shard_map/ppermute | solution.py:31
  44.1 0.5 fusion.1
  44.7 0.5 convolution_add_fusion.2
  45.2 1.9 %collective-permute-start.7 = (f32[128,1024]{1,0:T(8,128)S(1)}, f32[128,1024]{1,0:T(8,128)S(1)}, u32[]{:S(2)}, u32[]{:S(2)}) collective-permute-start(f32[128,1024]{1,0:T(8,128)S(1)} %pad_maximum_fusion), channel_id=1, source_target_pairs={{0,24},{8,16},{16,8},{24,0},{32,40},{40,32},{48,56},{56,48},{1,25}... | collective-permute-start | bytes 1572872 | tf_op jit(solution)/shard_map/ppermute | solution.py:31
  47.2 0.0 collective-permute-done.6
  47.2 0.5 fusion.7
  47.7 0.5 fusion.8
  48.2 0.0 collective-permute-done.1
  48.2 0.5 convolution_add_fusion.1
  48.8 0.5 convolution_add_fusion
  49.3 8.2 %collective-permute-done.7 = f32[128,1024]{1,0:T(8,128)S(1)} collective-permute-done((f32[128,1024]{1,0:T(8,128)S(1)}, f32[128,1024]{1,0:T(8,128)S(1)}, u32[]{:S(2)}, u32[]{:S(2)}) %collective-permute-start.7) | collective-permute-done | bytes 524320 | tf_op jit(solution)/shard_map/ppermute | solution.py:31
  57.5 0.1 maximum_add_fusion
  57.7 0.1 fusion
  57.8 22.7 %all_to_all.5 = f32[8,128,128]{2,1,0:T(8,128)S(1)} all-to-all(f32[8,128,128]{2,1,0:T(8,128)S(1)} %fusion), channel_id=1, replica_groups={{0,1,2,3,4,5,6,7},{8,9,10,11,12,13,14,15},{16,17,18,19,20,21,22,23},{24..., dimensions={0} | all-to-all | bytes 1048576 | tf_op jit(solution)/shard_map/all_to_all | solution.py:103
  80.6 4.2 %collective-permute-start.8 = (f32[128,128]{1,0:T(8,128)S(1)}, f32[128,128]{1,0:T(8,128)S(1)}, u32[]{:S(2)}, u32[]{:S(2)}) collective-permute-start(f32[128,128]{1,0:T(8,128)S(1)} %reduce_sum.9), channel_id=1, source_target_pairs={{0,128},{8,256},{16,384},{24,0},{64,448},{72,64},{80,192},{88,320}... | collective-permute-start | bytes 196616 | tf_op jit(solution)/shard_map/ppermute | solution.py:31
  84.7 8.0 %collective-permute-done.8 = f32[128,128]{1,0:T(8,128)S(1)} collective-permute-done((f32[128,128]{1,0:T(8,128)S(1)}, f32[128,128]{1,0:T(8,128)S(1)}, u32[]{:S(2)}, u32[]{:S(2)}) %collective-permute-start.8) | collective-permute-done | bytes 65568 | tf_op jit(solution)/shard_map/ppermute | solution.py:31
  92.7 0.6 copy.19
  (12 shorter events, 0.2 us)
Async XLA Ops:
  0.0 1.2 %copy-start.2 = (s32[6,4]{0,1:T(4,128)S(1)}, s32[6,4]{0,1:T(4,128)}, u32[]{:S(2)}) copy-start(s32[6,4]{0,1:T(4,128)} %param.7) | copy-start | bytes 292
  1.4 3.3 %copy-start.3 = (s32[2,6]{1,0:T(2,128)S(1)}, s32[2,6]{1,0:T(2,128)}, u32[]{:S(2)}) copy-start(s32[2,6]{1,0:T(2,128)} %param.6) | copy-start | bytes 148
  1.4 20.0 %collective-permute-start = (f32[384,256]{0,1:T(8,128)S(1)}, f32[384,256]{0,1:T(8,128)S(1)}, u32[]{:S(2)}, u32[]{:S(2)}) collective-permute-start(f32[384,256]{0,1:T(8,128)S(1)} %bitcast_multiply_fusion), channel_id=1, source_target_pairs={{0,64},{64,0},{1,65},{65,1},{2,66},{66,2},{3,67},{67,3},{4,68},{68... | collective-permute-start | bytes 1179656 | tf_op jit(solution)/shard_map/ppermute | solution.py:31
  5.0 0.9 copy-start.1
  5.9 19.9 %collective-permute-start.4 = (f32[128,384]{1,0:T(8,128)S(1)}, f32[128,384]{1,0:T(8,128)S(1)}, u32[]{:S(2)}, u32[]{:S(2)}) collective-permute-start(f32[128,384]{1,0:T(8,128)S(1)} %mul.9), channel_id=1, source_target_pairs={{0,0},{8,136},{16,272},{24,408},{32,288},{40,424},{48,48},{56,184}... | collective-permute-start | bytes 589832 | tf_op jit(solution)/shard_map/ppermute | solution.py:31
  13.3 14.2 %collective-permute-start.5 = (f32[128,384]{1,0:T(8,128)S(1)}, f32[128,384]{1,0:T(8,128)}, u32[]{:S(2)}, u32[]{:S(2)}) collective-permute-start(f32[128,384]{1,0:T(8,128)S(1)} %mul.9), channel_id=1, source_target_pairs={{0,136},{8,0},{16,408},{24,272},{32,184},{40,48},{48,424},{56,288}... | collective-permute-start | bytes 589832 | tf_op jit(solution)/shard_map/ppermute | solution.py:31
  17.6 17.3 %collective-permute-start.2 = (f32[384,512]{0,1:T(8,128)S(1)}, f32[384,512]{0,1:T(8,128)S(1)}, u32[]{:S(2)}, u32[]{:S(2)}) collective-permute-start(f32[384,512]{0,1:T(8,128)S(1)} %all_gather.7), channel_id=1, source_target_pairs={{0,8},{8,0},{16,24},{24,16},{32,56},{40,48},{48,40},{56,32},{1,9},... | collective-permute-start | bytes 2359304 | tf_op jit(solution)/shard_map/ppermute | solution.py:31
  23.8 20.3 %collective-permute-start.3 = (f32[384,512]{0,1:T(8,128)S(1)}, f32[384,512]{0,1:T(8,128)S(1)}, u32[]{:S(2)}, u32[]{:S(2)}) collective-permute-start(f32[384,512]{0,1:T(8,128)S(1)} %all_gather.6), channel_id=1, source_target_pairs={{0,8},{8,0},{16,24},{24,16},{32,56},{40,48},{48,40},{56,32},{1,9},... | collective-permute-start | bytes 2359304 | tf_op jit(solution)/shard_map/ppermute | solution.py:31
  25.8 1.7 %copy-start.4 = (f32[128,384]{1,0:T(8,128)}, f32[128,384]{1,0:T(8,128)S(1)}, u32[]{:S(2)}) copy-start(f32[128,384]{1,0:T(8,128)S(1)} %collective-permute-done.4.own_ref) | copy-start | bytes 589828
  29.3 7.1 %copy-start = (f32[128,768]{1,0:T(8,128)S(1)}, f32[128,768]{1,0:T(8,128)}, u32[]{:S(2)}) copy-start(f32[128,768]{1,0:T(8,128)} %shard_map.46) | copy-start | bytes 1179652
  29.3 17.8 %collective-permute-start.6 = (f32[128,384]{1,0:T(8,128)S(1)}, f32[128,384]{1,0:T(8,128)S(1)}, u32[]{:S(2)}, u32[]{:S(2)}) collective-permute-start(f32[128,384]{1,0:T(8,128)S(1)} %mul.9), channel_id=1, source_target_pairs={{0,264},{8,384},{16,24},{24,144},{32,56},{40,176},{48,296},{56,416... | collective-permute-start | bytes 589832 | tf_op jit(solution)/shard_map/ppermute | solution.py:31
  32.2 16.0 %collective-permute-start.1 = (f32[128,384]{1,0:T(8,128)S(1)}, f32[128,384]{1,0:T(8,128)S(1)}, u32[]{:S(2)}, u32[]{:S(2)}) collective-permute-start(f32[128,384]{1,0:T(8,128)S(1)} %mul.9), channel_id=1, source_target_pairs={{0,384},{8,264},{16,144},{24,24},{32,416},{40,296},{48,176},{56,56... | collective-permute-start | bytes 589832 | tf_op jit(solution)/shard_map/ppermute | solution.py:31
  45.2 12.3 %collective-permute-start.7 = (f32[128,1024]{1,0:T(8,128)S(1)}, f32[128,1024]{1,0:T(8,128)S(1)}, u32[]{:S(2)}, u32[]{:S(2)}) collective-permute-start(f32[128,1024]{1,0:T(8,128)S(1)} %pad_maximum_fusion), channel_id=1, source_target_pairs={{0,24},{8,16},{16,8},{24,0},{32,40},{40,32},{48,56},{56,48},{1,25}... | collective-permute-start | bytes 1572872 | tf_op jit(solution)/shard_map/ppermute | solution.py:31
  80.6 12.2 %collective-permute-start.8 = (f32[128,128]{1,0:T(8,128)S(1)}, f32[128,128]{1,0:T(8,128)S(1)}, u32[]{:S(2)}, u32[]{:S(2)}) collective-permute-start(f32[128,128]{1,0:T(8,128)S(1)} %reduce_sum.9), channel_id=1, source_target_pairs={{0,128},{8,256},{16,384},{24,0},{64,448},{72,64},{80,192},{88,320}... | collective-permute-start | bytes 196616 | tf_op jit(solution)/shard_map/ppermute | solution.py:31
